TPU v7x, 128 devices: a whole 4x4x4 slice. The times are simulated.
128 devices in a mesh: sx: 32 (over z, x, core), sy: 4 (over y).
Axes of the slice: x: 4, y: 4, z: 4, core: 2. Of those that a mesh axis runs over, the one named last changes fastest.
Arguments:
- rhs: float32 [512, 128, 512], P('sx', 'sy'), may hold values from -3 to 3.5
- perm_h: float32 [512, 128, 512], P('sx', 'sy'), may hold values from 0.05 to 20
- perm_v: float32 [512, 128, 512], P('sx', 'sy'), may hold values from 0.01 to 5
- prolong: float32 [2, 512, 128, 512], P(None, 'sx', 'sy'), may hold values from 0.2 to 1
- blk_slot: int32 [2, 512, 512], P(None, 'sx', 'sy'), may hold values from 0 to 2303, as said below
- recv_slot: int32 [2304, 128], P(None, ('sx', 'sy')), may hold values from 0 to 1024, as said below
- coarse_cols: int32 [8, 131072], P(None, ('sx', 'sy')), may hold values from 0 to 9215, as said below
- coarse_off: float32 [8, 131072], P(None, ('sx', 'sy')), may hold values from -0.11 to 0.04
- coarse_diag: float32 [1, 131072], P(None, ('sx', 'sy')), may hold values from 4 to 40
Outputs:
- pressure: float32 [512, 128, 512], P('sx', 'sy')
Inputs may be any that keep to these rules, and one draw needn't show every extreme that they name: `blk_slot`: each value names a non-empty entry of its source device's lists, only lists to owners that exist, and every non-empty entry is named by some block. `recv_slot`: the non-empty entries of one list come first and name distinct aggregates; 1024 marks an empty entry, and lists from sources outside the mesh are empty. A device's list to itself is full. `coarse_cols`: offsets name owners that exist.
All inputs are finite; a program needn't handle non-finite values.
Results may differ from a plain program's by a relative error of at most 0.0003.
Values sent between devices are 32-bit elements; how exact they have to be, the bound alone decides.
A program may use at most 192 MiB of HBM per device.

v0:
```python
import jax
import jax.numpy as jnp
from jax import lax
from jax.sharding import PartitionSpec as P

SWEEPS = 2
CYCLES = 2
CJ = 4


storage_coef = 0.01
cheb_low = 0.25
cheb_high = 2.0
omega = 0.8
highest = lax.Precision.HIGHEST


def with_halo(cells, sides, width):
    for axis, dim in sides:
        count = lax.axis_size(axis)
        ends = count - 1
        head = lax.slice_in_dim(cells, 0, width, axis=dim)
        tail = lax.slice_in_dim(cells, cells.shape[dim] - width, cells.shape[dim], axis=dim)
        cells = jnp.concatenate(
            [
                lax.ppermute(tail, axis, [(i, (i + 1) % count) for i in range(ends)]),
                cells,
                lax.ppermute(head, axis, [((i + 1) % count, i) for i in range(ends)]),
            ],
            axis=dim,
        )
    return cells


def safe_harmonic(left, right):
    total = left + right
    return 2.0 * left * right / (total + (total == 0.0).astype(jnp.float32))


def transmit(rim_h, core_v):
    core = rim_h[1:-1, 1:-1]
    t_east = safe_harmonic(core, rim_h[2:, 1:-1])
    t_west = safe_harmonic(core, rim_h[:-2, 1:-1])
    t_north = safe_harmonic(core, rim_h[1:-1, 2:])
    t_south = safe_harmonic(core, rim_h[1:-1, :-2])
    vertical = jnp.pad(core_v, ((0, 0), (0, 0), (1, 1)))
    t_up = safe_harmonic(core_v, vertical[:, :, 2:])
    t_down = safe_harmonic(core_v, vertical[:, :, :-2])
    diag = storage_coef + t_east + t_west + t_north + t_south + t_up + t_down
    return ((t_east, t_west, t_north, t_south, t_up, t_down), diag)


def fetch_near(iterate):
    grid = iterate.reshape(1, 1, -1)
    rimmed = with_halo(grid, (("sx", 0), ("sy", 1)), 1)
    return rimmed.reshape(-1)


def to_owners(outgoing, cap):
    grid = outgoing.reshape(3, 3, cap)
    rimmed = with_halo(grid, (("sx", 0), ("sy", 1)), 1)
    return rimmed[0::2, 0::2].reshape(-1)


def to_sources(reply, cap):
    grid = reply.reshape(3, 3, cap)
    rimmed = with_halo(grid, (("sx", 0), ("sy", 1)), 1)
    return rimmed[0::2, 0::2].reshape(-1)


def shards(rhs, perm_h, perm_v, prolong, blk_slot, recv_slot, coarse_cols, coarse_off, coarse_diag):
    cap = recv_slot.shape[0] // 9
    agg_dev = coarse_diag.shape[1]
    width_x, width_y, width_z = rhs.shape
    per_row = blk_slot.shape[2]
    offsets = jnp.arange(9, dtype=jnp.int32)
    theta = 0.5 * (cheb_high + cheb_low)
    delta = 0.5 * (cheb_high - cheb_low)
    sigma = theta / delta
    rimmed_perm = with_halo(perm_h, (("sx", 0), ("sy", 1)), 1)
    trans, diag = transmit(rimmed_perm, perm_v)

    def apply_region(field):
        t_east, t_west, t_north, t_south, t_up, t_down = [item for item in trans]
        core = field[1:-1, 1:-1]
        vertical = jnp.pad(core, ((0, 0), (0, 0), (1, 1)))
        out = diag * core - t_east * field[2:, 1:-1] - t_west * field[:-2, 1:-1]
        out = out - t_north * field[1:-1, 2:] - t_south * field[1:-1, :-2]
        return out - t_up * vertical[:, :, 2:] - t_down * vertical[:, :, :-2]

    def apply_op(field):
        rimmed = with_halo(field, (("sx", 0), ("sy", 1)), 1)
        return apply_region(rimmed)

    def smooth(pressure):
        rho = 1.0 / sigma
        scaled = (rhs - apply_op(pressure)) / diag
        update = scaled / theta
        for sweep in range(SWEEPS):
            pressure = pressure + update
            if sweep < SWEEPS - 1:
                scaled = (rhs - apply_op(pressure)) / diag
                rho_next = 1.0 / (2.0 * sigma - rho)
                update = rho_next * rho * update + 2.0 * rho_next / delta * scaled
                rho = rho_next
        return pressure

    flat_slot = blk_slot.reshape(-1)
    entry_hot = (flat_slot[:, None] % cap == jnp.arange(cap, dtype=jnp.int32)[None, :]).astype(
        jnp.float32
    )
    list_mask = (flat_slot[None, :] // cap == offsets[:, None]).astype(jnp.float32)
    recv_hot = (
        recv_slot.reshape(-1)[:, None] == jnp.arange(agg_dev, dtype=jnp.int32)[None, :]
    ).astype(jnp.float32)
    targets = offsets[:, None, None] * agg_dev + jnp.arange(agg_dev, dtype=jnp.int32)[None, None, :]
    coupling = jnp.zeros((9, agg_dev, agg_dev), jnp.float32)
    for term in range(coarse_cols.shape[0]):
        hits = (coarse_cols[term][None, :, None] == targets).astype(jnp.float32)
        coupling = coupling + coarse_off[term][None, :, None] * hits
    shaped = prolong.reshape(prolong.shape[0], width_x, per_row, 128)
    pressure = jnp.zeros_like(rhs)
    for cycle in range(CYCLES):
        pressure = smooth(pressure)
        resid = rhs - apply_op(pressure)
        partial_value = jnp.sum(shaped * resid.reshape(1, width_x, per_row, 128), axis=-1)
        outgoing = jnp.dot(
            list_mask * partial_value.reshape(-1)[None, :],
            entry_hot,
            precision=highest,
            preferred_element_type=jnp.float32,
        ).reshape(-1)
        arrived = to_owners(outgoing, cap)
        coarse_rhs = jnp.dot(
            arrived, recv_hot, precision=highest, preferred_element_type=jnp.float32
        )
        ratio = coarse_rhs / coarse_diag[0]
        iterate = omega * ratio
        for step in range(CJ):
            whole = fetch_near(iterate).reshape(9, agg_dev)
            coupled = jnp.einsum(
                "oga,oa->g", coupling, whole, precision=highest, preferred_element_type=jnp.float32
            )
            iterate = iterate + omega * (ratio - iterate - coupled)
        reply = jnp.dot(recv_hot, iterate, precision=highest, preferred_element_type=jnp.float32)
        correction_listed = to_sources(reply, cap)
        picked = jnp.dot(
            entry_hot,
            correction_listed.reshape(9, cap).T,
            precision=highest,
            preferred_element_type=jnp.float32,
        )
        values = jnp.sum(picked * list_mask.T, axis=1).reshape(partial_value.shape)
        pressure = pressure + jnp.sum(shaped * values[..., None], axis=0).reshape(
            width_x, width_y, width_z
        )
        pressure = smooth(pressure)
    return pressure


def solution(mesh):
    placed = (
        P("sx", "sy", None),
        P("sx", "sy", None),
        P("sx", "sy", None),
        P(None, "sx", "sy", None),
        P(None, "sx", "sy"),
        P(None, ("sx", "sy")),
        P(None, ("sx", "sy")),
        P(None, ("sx", "sy")),
        P(None, ("sx", "sy")),
    )
    return jax.shard_map(
        shards, mesh=mesh, in_specs=placed, out_specs=P("sx", "sy", None), check_vma=False
    )
```

profile of v0, /device:TPU:7, one launch (start us, length us, event | category | flops | bytes accessed | tf_op | source)
XLA Modules:
  0.0 811.9 jit_solution(16097809947185545086)
XLA Ops:
  9.2 5.5 collective-permute-start.1
  29.5 7.6 broadcast_multiply_fusion
  43.6 5.8 collective-permute-done.8
  64.5 5.1 collective-permute-done.12
  71.0 4.6 collective-permute-start.15
  78.8 8.1 fusion.40
  99.0 4.8 collective-permute-done.17
  117.0 5.8 collective-permute-start.20
  128.8 31.1 %select_add_fusion = f32[9,1024,1024]{2,1,0:T(8,128)} fusion(f32[1024]{0:T(1024)S(1)} %bitcast.138, f32[1024]{0:T(1024)S(1)} %bitcast.139, f32[1024]{0:T(1024)S(1)} %bitcast.133, f32[1024]{0:T(1024)S(1)} %bitcast.134, f32[1024]{0:T(1024)S(1)} %bitcast.135, f32[1024]{0:T(1024)S(1)} %bitcast.136, f32[1024]{0:T(1024)S(1)} %bitcast.137, f32[1024]{0:T(1024)S(1)} %bitcast.132, ...), kind=kLoop, calls=%fused_computation | loop fusion | flops 217055232 | bytes 37851136 | tf_op jit(solution)/shard_map/add | solution.py:120
  160.1 35.8 %fusion.209 = f32[1,1024,1]{1,0,2:T(1,128)S(1)} fusion(f32[9,1024,1024]{2,1,0:T(8,128)} %select_add_fusion, f32[9,1024,1]{1,2,0:T(1,128)S(1)} %reshape.264), kind=kOutput, calls=%fused_computation.419 | convolution fusion | flops 113246208 | bytes 37789696 | tf_op jit(solution)/shard_map/oga,oa->g/dot_general | solution.py:141
  197.8 6.9 collective-permute-start.24
  212.1 35.8 %fusion.210 = f32[1,1024,1]{1,0,2:T(1,128)S(1)} fusion(f32[9,1024,1024]{2,1,0:T(8,128)} %select_add_fusion, f32[9,1024,1]{1,2,0:T(1,128)S(1)} %reshape.266), kind=kOutput, calls=%fused_computation.420 | convolution fusion | flops 113246208 | bytes 37789696 | tf_op jit(solution)/shard_map/oga,oa->g/dot_general | solution.py:141
  249.8 7.4 collective-permute-start.28
  259.3 4.5 collective-permute-start.30
  264.8 35.8 %fusion.211 = f32[1,1024,1]{1,0,2:T(1,128)S(1)} fusion(f32[9,1024,1024]{2,1,0:T(8,128)} %select_add_fusion, f32[9,1024,1]{1,2,0:T(1,128)S(1)} %reshape.268), kind=kOutput, calls=%fused_computation.421 | convolution fusion | flops 113246208 | bytes 37789696 | tf_op jit(solution)/shard_map/oga,oa->g/dot_general | solution.py:141
  302.5 7.1 collective-permute-start.32
  311.7 4.7 collective-permute-start.34
  317.2 35.8 %fusion.212 = f32[1,1024,1]{1,0,2:T(1,128)S(1)} fusion(f32[9,1024,1024]{2,1,0:T(8,128)} %select_add_fusion, f32[9,1024,1]{1,2,0:T(1,128)S(1)} %reshape.270), kind=kOutput, calls=%fused_computation.422 | convolution fusion | flops 113246208 | bytes 37789696 | tf_op jit(solution)/shard_map/oga,oa->g/dot_general | solution.py:141
  357.5 7.1 collective-permute-start.36
  366.6 5.1 collective-permute-done.37
  396.9 5.8 collective-permute-done.40
  417.0 5.8 collective-permute-done.44
  424.1 4.6 collective-permute-start.47
  437.6 5.8 collective-permute-done.48
  444.7 4.6 collective-permute-start.51
  458.0 5.8 collective-permute-done.52
  465.1 4.6 collective-permute-start.55
  478.6 5.8 collective-permute-done.56
  485.7 4.6 collective-permute-start.59
  505.9 5.1 collective-permute-done.61
  524.8 5.8 collective-permute-start.64
  537.8 35.8 %fusion.213 = f32[1,1024,1]{1,0,2:T(1,128)S(1)} fusion(f32[9,1024,1024]{2,1,0:T(8,128)} %select_add_fusion, f32[9,1024,1]{1,2,0:T(1,128)S(1)} %reshape.274), kind=kOutput, calls=%fused_computation.423 | convolution fusion | flops 113246208 | bytes 37789696 | tf_op jit(solution)/shard_map/oga,oa->g/dot_general | solution.py:141
  575.5 7.2 collective-permute-start.68
  584.7 4.7 collective-permute-start.70
  590.2 35.8 %fusion.214 = f32[1,1024,1]{1,0,2:T(1,128)S(1)} fusion(f32[9,1024,1024]{2,1,0:T(8,128)} %select_add_fusion, f32[9,1024,1]{1,2,0:T(1,128)S(1)} %reshape.276), kind=kOutput, calls=%fused_computation.424 | convolution fusion | flops 113246208 | bytes 37789696 | tf_op jit(solution)/shard_map/oga,oa->g/dot_general | solution.py:141
  627.9 7.1 collective-permute-start.72
  637.1 4.5 collective-permute-start.74
  642.6 35.8 %fusion.215 = f32[1,1024,1]{1,0,2:T(1,128)S(1)} fusion(f32[9,1024,1024]{2,1,0:T(8,128)} %select_add_fusion, f32[9,1024,1]{1,2,0:T(1,128)S(1)} %reshape.278), kind=kOutput, calls=%fused_computation.425 | convolution fusion | flops 113246208 | bytes 37789696 | tf_op jit(solution)/shard_map/oga,oa->g/dot_general | solution.py:141
  680.3 7.1 collective-permute-start.76
  689.5 4.8 collective-permute-start.78
  695.0 35.8 %fusion.216 = f32[1,1024,1]{1,0,2:T(1,128)S(1)} fusion(f32[9,1024,1024]{2,1,0:T(8,128)} %select_add_fusion, f32[9,1024,1]{1,2,0:T(1,128)S(1)} %reshape.280), kind=kOutput, calls=%fused_computation.426 | convolution fusion | flops 113246208 | bytes 37789696 | tf_op jit(solution)/shard_map/oga,oa->g/dot_general | solution.py:141
  730.7 4.5 fusion.17
  735.3 7.1 collective-permute-start.80
  744.4 5.1 collective-permute-done.81
  774.7 5.8 collective-permute-done.84
  781.8 4.5 collective-permute-start.87
  794.8 5.8 collective-permute-done.88
  801.9 4.6 collective-permute-start.91
  (320 shorter events, 271.4 us)
Async XLA Ops:
  0.0 14.7 %collective-permute-start.5 = (f32[1,32,512]{2,1,0:T(8,128)S(1)}, f32[1,32,512]{2,1,0:T(8,128)S(1)}, u32[]{:S(2)}, u32[]{:S(2)}) collective-permute-start(f32[1,32,512]{2,1,0:T(8,128)S(1)} %broadcast.164), channel_id=1, source_target_pairs={{0,4},{4,8},{8,12},{12,16},{16,20},{20,24},{24,28},{28,32},{32,36}... | collective-permute-start | bytes 196616 | tf_op jit(solution)/shard_map/ppermute | solution.py:26
  4.2 10.5 %collective-permute-start.4 = (f32[1,32,512]{2,1,0:T(8,128)S(1)}, f32[1,32,512]{2,1,0:T(8,128)S(1)}, u32[]{:S(2)}, u32[]{:S(2)}) collective-permute-start(f32[1,32,512]{2,1,0:T(8,128)S(1)} %broadcast.164), channel_id=1, source_target_pairs={{4,0},{8,4},{12,8},{16,12},{20,16},{24,20},{28,24},{32,28},{36,32}... | collective-permute-start | bytes 196616 | tf_op jit(solution)/shard_map/ppermute | solution.py:28
  7.0 14.5 %collective-permute-start = (f32[1,32,512]{2,1,0:T(8,128)S(1)}, f32[1,32,512]{2,1,0:T(8,128)S(1)}, u32[]{:S(2)}, u32[]{:S(2)}) collective-permute-start(f32[1,32,512]{2,1,0:T(8,128)S(1)} %get-tuple-element.61), channel_id=1, source_target_pairs={{4,0},{8,4},{12,8},{16,12},{20,16},{24,20},{28,24},{32,28},{36,32}... | collective-permute-start | bytes 196616 | tf_op jit(solution)/shard_map/ppermute | solution.py:28
  9.2 11.0 %collective-permute-start.1 = (f32[1,32,512]{2,1,0:T(8,128)S(1)}, f32[1,32,512]{2,1,0:T(8,128)S(1)}, u32[]{:S(2)}, u32[]{:S(2)}) collective-permute-start(f32[1,32,512]{2,1,0:T(8,128)S(1)} %get-tuple-element.62), channel_id=1, source_target_pairs={{0,4},{4,8},{8,12},{12,16},{16,20},{20,24},{24,28},{28,32},{32,36}... | collective-permute-start | bytes 196616 | tf_op jit(solution)/shard_map/ppermute | solution.py:26
  14.9 11.2 %collective-permute-start.6 = (f32[18,1,512]{2,1,0:T(1,128)S(1)}, f32[18,1,512]{2,1,0:T(1,128)S(1)}, u32[]{:S(2)}, u32[]{:S(2)}) collective-permute-start(f32[18,1,512]{2,1,0:T(1,128)S(1)} %get-tuple-element.41), channel_id=1, source_target_pairs={{1,0},{2,1},{3,2},{5,4},{6,5},{7,6},{9,8},{10,9},{11,10},{13,12},{... | collective-permute-start | bytes 110600 | tf_op jit(solution)/shard_map/ppermute | solution.py:28
  16.2 10.0 %collective-permute-start.7 = (f32[18,1,512]{2,1,0:T(1,128)S(1)}, f32[18,1,512]{2,1,0:T(1,128)S(1)}, u32[]{:S(2)}, u32[]{:S(2)}) collective-permute-start(f32[18,1,512]{2,1,0:T(1,128)S(1)} %get-tuple-element.42), channel_id=1, source_target_pairs={{0,1},{1,2},{2,3},{4,5},{5,6},{6,7},{8,9},{9,10},{10,11},{12,13},{... | collective-permute-start | bytes 110600 | tf_op jit(solution)/shard_map/ppermute | solution.py:26
  37.2 6.3 collective-permute-start.9
  41.6 7.7 collective-permute-start.8
  61.9 7.7 collective-permute-start.12
  69.7 9.1 %collective-permute-start.14 = (f32[18,1,512]{2,1,0:T(1,128)S(1)}, f32[18,1,512]{2,1,0:T(1,128)S(1)}, u32[]{:S(2)}, u32[]{:S(2)}) collective-permute-start(f32[18,1,512]{2,1,0:T(1,128)S(1)} %get-tuple-element.35), channel_id=1, source_target_pairs={{1,0},{2,1},{3,2},{5,4},{6,5},{7,6},{9,8},{10,9},{11,10},{13,12},{... | collective-permute-start | bytes 110600 | tf_op jit(solution)/shard_map/ppermute | solution.py:28
  71.0 7.8 collective-permute-start.15
  96.8 7.0 collective-permute-start.17
  103.8 5.9 collective-permute-start.18
  115.1 7.7 collective-permute-start.21
  117.0 6.5 collective-permute-start.20
  123.6 36.4 %collective-permute-start.23 = (f32[3,1,1024]{2,1,0:T(1,128)S(1)}, f32[3,1,1024]{2,1,0:T(1,128)S(1)}, u32[]{:S(2)}, u32[]{:S(2)}) collective-permute-start(f32[3,1,1024]{2,1,0:T(1,128)S(1)} %pad_maximum_fusion.124), channel_id=1, source_target_pairs={{1,0},{2,1},{3,2},{5,4},{6,5},{7,6},{9,8},{10,9},{11,10},{13,12},{... | collective-permute-start | bytes 36872 | tf_op jit(solution)/shard_map/ppermute | solution.py:28
  124.9 35.1 %collective-permute-start.22 = (f32[3,1,1024]{2,1,0:T(1,128)S(1)}, f32[3,1,1024]{2,1,0:T(1,128)S(1)}, u32[]{:S(2)}, u32[]{:S(2)}) collective-permute-start(f32[3,1,1024]{2,1,0:T(1,128)S(1)} %pad_maximum_fusion.124), channel_id=1, source_target_pairs={{0,1},{1,2},{2,3},{4,5},{5,6},{6,7},{8,9},{9,10},{10,11},{12,13},{... | collective-permute-start | bytes 36872 | tf_op jit(solution)/shard_map/ppermute | solution.py:26
  195.9 8.8 %collective-permute-start.25 = (f32[1,1,1024]{2,1,0:T(1,128)S(1)}, f32[1,1,1024]{2,1,0:T(1,128)S(1)}, u32[]{:S(2)}, u32[]{:S(2)}) collective-permute-start(f32[1,1,1024]{2,1,0:T(1,128)S(1)} %bitcast.98), channel_id=1, source_target_pairs={{4,0},{8,4},{12,8},{16,12},{20,16},{24,20},{28,24},{32,28},{36,32}... | collective-permute-start | bytes 12296 | tf_op jit(solution)/shard_map/ppermute | solution.py:28
  197.8 7.6 collective-permute-start.24
  247.9 9.4 %collective-permute-start.29 = (f32[1,1,1024]{2,1,0:T(1,128)S(1)}, f32[1,1,1024]{2,1,0:T(1,128)S(1)}, u32[]{:S(2)}, u32[]{:S(2)}) collective-permute-start(f32[1,1,1024]{2,1,0:T(1,128)S(1)} %bitcast.86), channel_id=1, source_target_pairs={{4,0},{8,4},{12,8},{16,12},{20,16},{24,20},{28,24},{32,28},{36,32}... | collective-permute-start | bytes 12296 | tf_op jit(solution)/shard_map/ppermute | solution.py:28
  249.8 8.2 %collective-permute-start.28 = (f32[1,1,1024]{2,1,0:T(1,128)S(1)}, f32[1,1,1024]{2,1,0:T(1,128)S(1)}, u32[]{:S(2)}, u32[]{:S(2)}) collective-permute-start(f32[1,1,1024]{2,1,0:T(1,128)S(1)} %bitcast.87), channel_id=1, source_target_pairs={{0,4},{4,8},{8,12},{12,16},{16,20},{20,24},{24,28},{28,32},{32,36}... | collective-permute-start | bytes 12296 | tf_op jit(solution)/shard_map/ppermute | solution.py:26
  300.5 9.1 %collective-permute-start.33 = (f32[1,1,1024]{2,1,0:T(1,128)S(1)}, f32[1,1,1024]{2,1,0:T(1,128)S(1)}, u32[]{:S(2)}, u32[]{:S(2)}) collective-permute-start(f32[1,1,1024]{2,1,0:T(1,128)S(1)} %bitcast.82), channel_id=1, source_target_pairs={{4,0},{8,4},{12,8},{16,12},{20,16},{24,20},{28,24},{32,28},{36,32}... | collective-permute-start | bytes 12296 | tf_op jit(solution)/shard_map/ppermute | solution.py:28
  302.5 7.9 collective-permute-start.32
  310.4 6.0 collective-permute-start.35
  357.5 9.1 %collective-permute-start.36 = (f32[1,3,256]{2,1,0:T(4,128)S(1)}, f32[1,3,256]{2,1,0:T(4,128)S(1)}, u32[]{:S(2)}, u32[]{:S(2)}) collective-permute-start(f32[1,3,256]{2,1,0:T(4,128)S(1)} %slice.594), channel_id=1, source_target_pairs={{0,4},{4,8},{8,12},{12,16},{16,20},{20,24},{24,28},{28,32},{32,36}... | collective-permute-start | bytes 9224 | tf_op jit(solution)/shard_map/ppermute | solution.py:26
  364.7 7.0 collective-permute-start.37
  394.9 7.7 collective-permute-start.40
  415.1 7.7 collective-permute-start.44
  422.8 5.9 collective-permute-start.46
  435.6 7.7 collective-permute-start.48
  456.1 7.7 collective-permute-start.52
  476.6 7.7 collective-permute-start.56
  504.0 7.0 collective-permute-start.61
  522.9 7.7 collective-permute-start.65
  524.8 6.5 collective-permute-start.64
  573.6 9.1 %collective-permute-start.69 = (f32[1,1,1024]{2,1,0:T(1,128)S(1)}, f32[1,1,1024]{2,1,0:T(1,128)S(1)}, u32[]{:S(2)}, u32[]{:S(2)}) collective-permute-start(f32[1,1,1024]{2,1,0:T(1,128)S(1)} %bitcast.102), channel_id=1, source_target_pairs={{4,0},{8,4},{12,8},{16,12},{20,16},{24,20},{28,24},{32,28},{36,32}... | collective-permute-start | bytes 12296 | tf_op jit(solution)/shard_map/ppermute | solution.py:28
  575.5 7.9 collective-permute-start.68
  583.4 6.0 collective-permute-start.71
  626.0 9.1 %collective-permute-start.73 = (f32[1,1,1024]{2,1,0:T(1,128)S(1)}, f32[1,1,1024]{2,1,0:T(1,128)S(1)}, u32[]{:S(2)}, u32[]{:S(2)}) collective-permute-start(f32[1,1,1024]{2,1,0:T(1,128)S(1)} %bitcast.90), channel_id=1, source_target_pairs={{4,0},{8,4},{12,8},{16,12},{20,16},{24,20},{28,24},{32,28},{36,32}... | collective-permute-start | bytes 12296 | tf_op jit(solution)/shard_map/ppermute | solution.py:28
  627.9 7.9 collective-permute-start.72
  678.4 9.1 %collective-permute-start.77 = (f32[1,1,1024]{2,1,0:T(1,128)S(1)}, f32[1,1,1024]{2,1,0:T(1,128)S(1)}, u32[]{:S(2)}, u32[]{:S(2)}) collective-permute-start(f32[1,1,1024]{2,1,0:T(1,128)S(1)} %bitcast.78), channel_id=1, source_target_pairs={{4,0},{8,4},{12,8},{16,12},{20,16},{24,20},{28,24},{32,28},{36,32}... | collective-permute-start | bytes 12296 | tf_op jit(solution)/shard_map/ppermute | solution.py:28
  680.3 7.9 collective-permute-start.76
  688.2 6.1 collective-permute-start.79
  735.3 9.1 %collective-permute-start.80 = (f32[1,3,256]{2,1,0:T(4,128)S(1)}, f32[1,3,256]{2,1,0:T(4,128)S(1)}, u32[]{:S(2)}, u32[]{:S(2)}) collective-permute-start(f32[1,3,256]{2,1,0:T(4,128)S(1)} %slice.658), channel_id=1, source_target_pairs={{0,4},{4,8},{8,12},{12,16},{16,20},{20,24},{24,28},{28,32},{32,36}... | collective-permute-start | bytes 9224 | tf_op jit(solution)/shard_map/ppermute | solution.py:26
  742.5 7.0 collective-permute-start.81
  772.7 7.7 collective-permute-start.84
  792.9 7.7 collective-permute-start.88
  800.6 5.9 collective-permute-start.90
  (63 other events, 840.8 us)
where the time goes:
time: 823 us; the launch traced here: 812 us
  matrix products  309 us (38%)
  starting transfers between devices  285 us (35%)
  waiting for transfers between devices  105 us (13%)
  other arithmetic  90.5 us (11%)
  local copies, waits for them, and re-layouts  20.3 us (2%)
    dot_general x8, matrix products, shards(): jnp.einsum('oga,oa->g', coupling, whole, precision=highest, preferred_ele...  286 us
    ppermute x46, starting transfers between devices, with_halo(): lax.ppermute(tail, axis, [(i, (i + 1) % count) for i in range(ends)])  210 us
    ppermute x46, waiting for transfers between devices, with_halo(): lax.ppermute(head, axis, [((i + 1) % count, i) for i in range(ends)])  86.3 us
    ppermute x46, starting transfers between devices, with_halo(): lax.ppermute(head, axis, [((i + 1) % count, i) for i in range(ends)])  75.1 us
    add x1, other arithmetic, shards(): coupling = coupling + coarse_off[term][None, :, None] * hits  31.1 us
    add x7, other arithmetic, smooth(): pressure = pressure + update  22.2 us
    ppermute x46, waiting for transfers between devices, with_halo(): lax.ppermute(tail, axis, [(i, (i + 1) % count) for i in range(ends)])  18.6 us
  transfers between devices with their start and end apart: 92, of which 41 were waited for; matrix products, arithmetic and copies ran while one was open for 5% of the time, Pallas kernels for 0%

commit v1 on v0

v1 whole, which is shorter than its diff:
```python
import functools

import jax
import jax.numpy as jnp
from jax import lax
from jax.experimental import pallas as pl
from jax.experimental.pallas import tpu as pltpu
from jax.sharding import PartitionSpec as P

CYCLES = 2
CJ = 4

storage_coef = 0.01
cheb_low = 0.25
cheb_high = 2.0
omega = 0.8

THETA = 0.5 * (cheb_high + cheb_low)
DELTA = 0.5 * (cheb_high - cheb_low)
SIGMA = THETA / DELTA
RHO0 = 1.0 / SIGMA
RHO1 = 1.0 / (2.0 * SIGMA - RHO0)
ALPHA = RHO1 * RHO0
BETA = 2.0 * RHO1 / DELTA

W = 5
T = 8
NX, NY, NZ = 16, 32, 512
TILES = (NY + 2 * T) // 8
MESH = pl.DeviceIdType.MESH
AROUND = (0, 1, 2, 3, 5, 6, 7, 8)
f32 = jnp.float32


def neighbour(o):
    x = lax.axis_index("sx") + (o // 3 - 1)
    y = lax.axis_index("sy") + (o % 3 - 1)
    there = (x >= 0) & (x < lax.axis_size("sx")) & (y >= 0) & (y < lax.axis_size("sy"))
    return x, y, there


def inverse(value):
    guess = pl.reciprocal(value, approx=True)
    return guess * (2.0 - value * guess)


def harmonic(left, right):
    total = left + right
    return 2.0 * left * right * inverse(jnp.where(total == 0.0, 1.0, total))


def kernel(
    rhs_h, ph_h, pv_h, pr_h, slot_r, recv_r, cols_r, off_r, diag_r, out_h,
    RHS, PH, PV, TE, TN, TU, INV, P0, P1, PR, ZH, ZL, HOT, SLOT, LT, VT, RIDX, INVL,
    OUT, ARR, TAB, REP, LIST, DIA, RAT, Y,
    in_sem, ssem, rsem, csend, crecv,
):
    sub = lax.broadcasted_iota(jnp.int32, (8, 128), 0)
    lane = lax.broadcasted_iota(jnp.int32, (8, 128), 1)
    lane512 = lax.broadcasted_iota(jnp.int32, (8, NZ), 1)

    def rows(j):
        return slice(8 * j, 8 * j + 8)

    center = (slice(W, W + NX), slice(T, T + NY), slice(None))
    loads = [
        pltpu.make_async_copy(src, dst, in_sem.at[n])
        for n, (src, dst) in enumerate(
            [(ph_h, PH.at[center]), (pv_h, PV.at[center]), (rhs_h, RHS.at[center]), (pr_h, PR)]
        )
    ]
    for load in loads:
        load.start()

    bar = pltpu.get_barrier_semaphore()
    for o in AROUND:
        x, y, there = neighbour(o)

        @pl.when(there)
        def _():
            pl.semaphore_signal(bar, inc=1, device_id=(x, y), device_id_type=MESH)

    for array in (PH, PV, RHS, P0):
        for o, strip in ((1, (slice(0, W),)), (7, (slice(W + NX, 2 * W + NX),)),
                         (3, (slice(None), slice(0, T))), (5, (slice(None), slice(T + NY, 2 * T + NY)))):
            _, _, there = neighbour(o)

            @pl.when(jnp.logical_not(there))
            def _():
                view = array.at[strip]
                count = view.shape[0]

                def clear(i, carry):
                    view[i] = jnp.zeros(view.shape[1:], f32)
                    return carry

                lax.fori_loop(0, count, clear, 0)

    peers = sum(neighbour(o)[2].astype(jnp.int32) for o in AROUND)
    pl.semaphore_wait(bar, peers)

    def strip_copies(n, dst, src, base_x, base_y):
        out = []
        for o in AROUND:
            dx, dy = o // 3 - 1, o % 3 - 1
            sx = {-1: (0, W), 0: (0, NX), 1: (NX - W, W)}[dx]
            tx = {-1: W + NX, 0: W, 1: 0}[dx]
            sy = {-1: (0, T), 0: (0, NY), 1: (NY - T, T)}[dy]
            ty = {-1: T + NY, 0: T, 1: 0}[dy]
            x, y, there = neighbour(o)
            copy = pltpu.make_async_remote_copy(
                src.at[pl.ds(base_x + sx[0], sx[1]), pl.ds(base_y + sy[0], sy[1]), :],
                dst.at[pl.ds(tx, sx[1]), pl.ds(ty, sy[1]), :],
                ssem.at[n, o], rsem.at[n, 8 - o], device_id=(x, y), device_id_type=MESH,
            )
            rx = {-1: 0, 0: W, 1: W + NX}[dx]
            ry = {-1: 0, 0: T, 1: T + NY}[dy]
            here = dst.at[pl.ds(rx, sx[1]), pl.ds(ry, sy[1]), :]
            arrive = pltpu.make_async_remote_copy(
                here, here, ssem.at[n, o], rsem.at[n, o], device_id=(x, y), device_id_type=MESH,
            )
            out.append((there, copy, arrive))
        return out

    def go(copies):
        for there, copy, _ in copies:
            @pl.when(there)
            def _():
                copy.start()

    def land(copies):
        for there, copy, arrive in copies:
            @pl.when(there)
            def _():
                arrive.wait_recv()
                copy.wait_send()

    first = [strip_copies(n, dst, src, 0, 0) for n, (dst, src) in enumerate([(PH, ph_h), (PV, pv_h), (RHS, rhs_h)])]
    for copies in first:
        go(copies)

    for k in range(2):
        for x8 in range(2):
            raw = slot_r[k, 8 * x8:8 * x8 + 8, :]
            order = (((lane >> 5) << 3) + (lane & 7)) * 4 + ((lane >> 3) & 3)
            SLOT[pl.ds(16 * k + 8 * x8, 8), :] = jnp.take_along_axis(
                raw, order, axis=1, mode="promise_in_bounds"
            )
    LT[...] = jnp.zeros_like(LT)
    LT[0:32, :] = SLOT[...] & 127
    LT[...] = LT[...].T
    row32 = lax.broadcasted_iota(jnp.int32, (32, 128), 0)
    for kx in range(32):
        line = jnp.broadcast_to(SLOT[kx:kx + 1, :] >> 7, (32, 128))
        HOT[:, kx * 128:(kx + 1) * 128] = (line == row32).astype(f32).astype(jnp.bfloat16)
    RIDX[...] = jnp.full_like(RIDX, 1024)
    for r in range(18):
        RIDX[r:r + 1, :] = recv_r[0:1, r * 128:(r + 1) * 128]
    low = lax.broadcasted_iota(jnp.int32, (128, 128), 0)
    cnum = lax.broadcasted_iota(jnp.int32, (8, 128), 1).astype(f32) + 1.0
    for o in range(9):
        total = jnp.zeros((8, 128), f32)
        for h in range(2):
            ids = RIDX[2 * o + h:2 * o + h + 1, :]
            a = jnp.where(jnp.broadcast_to(ids >> 7, (8, 128)) == sub, cnum + 128.0 * h, 0.0)
            b = (jnp.broadcast_to(ids & 127, (128, 128)) == low).astype(f32)
            total = total + lax.dot_general(
                a.astype(jnp.bfloat16), b.astype(jnp.bfloat16), (((1,), (1,)), ((), ())),
                preferred_element_type=f32,
            )
        INVL[o] = (total + 0.5).astype(jnp.int32) - 1
    for m in range(8):
        DIA[m:m + 1, :] = diag_r[0:1, m * 128:(m + 1) * 128]
    DIA[...] = 1.0 / DIA[...]

    for load in loads:
        load.wait()
    for copies in first:
        land(copies)

    def edge_x(i, carry):
        for j in range(TILES):
            TE[i, rows(j), :] = harmonic(PH[i, rows(j), :], PH[i + 1, rows(j), :])
        return carry

    lax.fori_loop(0, 2 * W + NX - 1, edge_x, 0)

    sub512 = lax.broadcasted_iota(jnp.int32, (8, NZ), 0)

    def edge_yz(i, carry):
        before = None
        for j in range(TILES):
            ctr = PH[i, rows(j), :]
            if j < TILES - 1:
                up = PH[i, 8 * j + 1:8 * j + 9, :]
            else:
                up = pltpu.roll(ctr, 7, 0)
            tn = harmonic(ctr, up)
            TN[i, rows(j), :] = tn
            pv = PV[i, rows(j), :]
            tu = jnp.where(lane512 == NZ - 1, 0.0, harmonic(pv, pltpu.roll(pv, NZ - 1, 1)))
            TU[i, rows(j), :] = tu
            rolled = pltpu.roll(tn, 1, 0)
            down = rolled if before is None else jnp.where(sub512 == 0, before, rolled)
            before = rolled
            total = storage_coef + TE[i, rows(j), :] + TE[i - 1, rows(j), :] + tn + down + tu + pltpu.roll(tu, 1, 1)
            INV[i, rows(j), :] = inverse(total)
        return carry

    lax.fori_loop(1, 2 * W + NX - 1, edge_yz, 0)

    def residual(field, i, j):
        ctr = field[i, rows(j), :]
        acc = RHS[i, rows(j), :] - storage_coef * ctr
        acc = acc + TE[i, rows(j), :] * (field[i + 1, rows(j), :] - ctr)
        acc = acc + TE[i - 1, rows(j), :] * (field[i - 1, rows(j), :] - ctr)
        fz = TU[i, rows(j), :] * (pltpu.roll(ctr, NZ - 1, 1) - ctr)
        acc = acc + fz - pltpu.roll(fz, 1, 1)
        if j < TILES - 1:
            up = field[i, 8 * j + 1:8 * j + 9, :]
        else:
            up = pltpu.roll(ctr, 7, 0)
        fn = TN[i, rows(j), :] * (up - ctr)
        if j > 0:
            fs = TN[i, 8 * j - 1:8 * j + 7, :] * (ctr - field[i, 8 * j - 1:8 * j + 7, :])
        else:
            fs = pltpu.roll(fn, 1, 0)
        return ctr, acc + fn - fs

    def sweep(extent, update):
        tiles = range(TILES) if extent > 0 else range(1, TILES - 1)

        def body(i, carry):
            for j in tiles:
                update(i, j)
            return carry

        lax.fori_loop(W - extent, W + NX + extent, body, 0)

    def start_from_zero(i, j):
        P1[i, rows(j), :] = (1.0 / THETA) * INV[i, rows(j), :] * RHS[i, rows(j), :]

    def sweep_a(i, j):
        ctr, res = residual(P0, i, j)
        P1[i, rows(j), :] = ctr + (1.0 / THETA) * INV[i, rows(j), :] * res

    def sweep_b_first(i, j):
        ctr, res = residual(P1, i, j)
        P0[i, rows(j), :] = (1.0 + ALPHA) * ctr + BETA * INV[i, rows(j), :] * res

    def sweep_b(i, j):
        ctr, res = residual(P1, i, j)
        P0[i, rows(j), :] = (1.0 + ALPHA) * ctr - ALPHA * P0[i, rows(j), :] + BETA * INV[i, rows(j), :] * res

    def restrict(i, carry):
        x = i - W
        for j in range(1, TILES - 1):
            _, res = residual(P0, i, j)
            t = j - 1
            for k in range(2):
                scaled = PR[k, x, 8 * t:8 * t + 8, :] * res
                which = jnp.full((8, 128), 16 * k, jnp.int32) + x
                pieces = []
                for zb in range(4):
                    part = jnp.sum(scaled[:, 128 * zb:128 * zb + 128], axis=1, keepdims=True)
                    b0 = (t * 4 + zb) * 8
                    at = jnp.take_along_axis(LT[b0:b0 + 8, :], which, axis=1, mode="promise_in_bounds")
                    pieces.append(jnp.where(at == lane, jnp.broadcast_to(part, (8, 128)), 0.0))
                for h in range(2):
                    both = jnp.concatenate(pieces[2 * h:2 * h + 2], axis=0)
                    high = both.astype(jnp.bfloat16)
                    at = pl.multiple_of((16 * k + x) * 128, 128) + (t * 4 + 2 * h) * 8
                    at = pl.multiple_of(at, 16)
                    ZH[pl.ds(at, 16), :] = high
                    ZL[pl.ds(at, 16), :] = (both - high.astype(f32)).astype(jnp.bfloat16)
        return carry

    def exchange(parity, src_of, dst):
        out = []
        for o in AROUND:
            x, y, there = neighbour(o)
            copy = pltpu.make_async_remote_copy(
                src_of(o), dst.at[8 - o], csend.at[parity, o], crecv.at[parity, 8 - o],
                device_id=(x, y), device_id_type=MESH,
            )
            arrive = pltpu.make_async_remote_copy(
                dst.at[o], dst.at[o], csend.at[parity, o], crecv.at[parity, o],
                device_id=(x, y), device_id_type=MESH,
            )
            out.append((there, copy, arrive))
        return out

    def coarse():
        listed = jnp.dot(HOT[...], ZH[...], preferred_element_type=f32) + jnp.dot(
            HOT[...], ZL[...], preferred_element_type=f32
        )
        for r in range(18):
            OUT[r // 2, r % 2:r % 2 + 1, :] = listed[r:r + 1, :]
        step = exchange(0, lambda o: OUT.at[o], ARR)
        go(step)
        ARR[4] = OUT[4]
        land(step)
        total = jnp.zeros((8, 128), f32)
        for o in range(9):
            at = INVL[o]
            for h in range(2):
                got = jnp.take_along_axis(
                    jnp.broadcast_to(ARR[o, h:h + 1, :], (8, 128)), at & 127, axis=1, mode="promise_in_bounds"
                )
                total = total + jnp.where((at >> 7) == h, got, 0.0)
        RAT[...] = total * DIA[...]
        Y[...] = omega * RAT[...]
        for s in range(CJ):
            table = TAB.at[s % 2]
            step = exchange((s + 1) % 2, lambda o: Y, table)
            go(step)
            table[4] = Y[...]
            land(step)
            for m in range(8):
                at = cols_r[:, 128 * m:128 * m + 128]
                got = jnp.zeros((8, 128), f32)
                for r in range(72):
                    one = jnp.take_along_axis(
                        jnp.broadcast_to(table[r // 8, r % 8:r % 8 + 1, :], (8, 128)), at & 127,
                        axis=1, mode="promise_in_bounds",
                    )
                    got = jnp.where((at >> 7) == r, one, got)
                coupled = jnp.sum(got * off_r[:, 128 * m:128 * m + 128], axis=0, keepdims=True)
                mine = Y[m:m + 1, :]
                Y[m:m + 1, :] = mine + omega * (RAT[m:m + 1, :] - mine - coupled)
        for r3 in range(3):
            at = RIDX[8 * r3:8 * r3 + 8, :]
            got = jnp.zeros((8, 128), f32)
            for r in range(8):
                one = jnp.take_along_axis(
                    jnp.broadcast_to(Y[r:r + 1, :], (8, 128)), at & 127, axis=1, mode="promise_in_bounds"
                )
                got = jnp.where((at >> 7) == r, one, got)
            for s in range(8):
                r = 8 * r3 + s
                if r < 18:
                    REP[r // 2, r % 2:r % 2 + 1, :] = got[s:s + 1, :]
        step = exchange((CJ + 1) % 2, lambda o: REP.at[o], LIST)
        go(step)
        LIST[4] = REP[4]
        land(step)
        VT[...] = jnp.zeros_like(VT)
        for r4 in range(4):
            at = SLOT[8 * r4:8 * r4 + 8, :]
            got = jnp.zeros((8, 128), f32)
            for r in range(18):
                one = jnp.take_along_axis(
                    jnp.broadcast_to(LIST[r // 2, r % 2:r % 2 + 1, :], (8, 128)), at & 127,
                    axis=1, mode="promise_in_bounds",
                )
                got = jnp.where((at >> 7) == r, one, got)
            VT[8 * r4:8 * r4 + 8, :] = got
        VT[...] = VT[...].T

        def correct(x, carry):
            for t in range(4):
                total = P0[x + W, T + 8 * t:T + 8 * t + 8, :]
                for k in range(2):
                    which = jnp.full((8, 128), 16 * k, jnp.int32) + x
                    spread = []
                    for zb in range(4):
                        b0 = (t * 4 + zb) * 8
                        spread.append(
                            jnp.take_along_axis(VT[b0:b0 + 8, :], which, axis=1, mode="promise_in_bounds")
                        )
                    total = total + PR[k, x, 8 * t:8 * t + 8, :] * jnp.concatenate(spread, axis=1)
                P0[x + W, T + 8 * t:T + 8 * t + 8, :] = total
            return carry

        lax.fori_loop(0, NX, correct, 0)

    for cycle in range(CYCLES):
        if cycle == 0:
            sweep(2, start_from_zero)
            sweep(1, sweep_b_first)
        else:
            sweep(2, sweep_a)
            sweep(1, sweep_b)
        lax.fori_loop(W, W + NX, restrict, 0)
        coarse()
        step = strip_copies(3 + cycle, P0, P0, W, T)
        go(step)
        land(step)
        if cycle == 0:
            sweep(4, sweep_a)
            sweep(3, sweep_b)
        else:
            sweep(1, sweep_a)
            sweep(0, sweep_b)
    back = pltpu.make_async_copy(P0.at[center], out_h, in_sem.at[0])
    back.start()
    back.wait()


def shards(rhs, perm_h, perm_v, prolong, blk_slot, recv_slot, coarse_cols, coarse_off, coarse_diag):
    padded = pltpu.VMEM((2 * W + NX, 2 * T + NY, NZ), f32)
    hbm = pl.BlockSpec(memory_space=pl.ANY)
    vmem = pl.BlockSpec(memory_space=pltpu.VMEM)
    return pl.pallas_call(
        kernel,
        out_shape=jax.ShapeDtypeStruct(rhs.shape, f32),
        in_specs=[hbm] * 4 + [vmem] * 5,
        out_specs=hbm,
        scratch_shapes=[padded] * 9
        + [
            pltpu.VMEM((2, NX, NY, NZ), f32),
            pltpu.VMEM((4096, 128), jnp.bfloat16),
            pltpu.VMEM((4096, 128), jnp.bfloat16),
            pltpu.VMEM((32, 4096), jnp.bfloat16),
            pltpu.VMEM((32, 128), jnp.int32),
            pltpu.VMEM((128, 128), jnp.int32),
            pltpu.VMEM((128, 128), f32),
            pltpu.VMEM((24, 128), jnp.int32),
            pltpu.VMEM((9, 8, 128), jnp.int32),
            pltpu.VMEM((9, 2, 128), f32),
            pltpu.VMEM((9, 2, 128), f32),
            pltpu.VMEM((2, 9, 8, 128), f32),
            pltpu.VMEM((9, 2, 128), f32),
            pltpu.VMEM((9, 2, 128), f32),
            pltpu.VMEM((8, 128), f32),
            pltpu.VMEM((8, 128), f32),
            pltpu.VMEM((8, 128), f32),
            pltpu.SemaphoreType.DMA((4,)),
            pltpu.SemaphoreType.DMA((5, 9)),
            pltpu.SemaphoreType.DMA((5, 9)),
            pltpu.SemaphoreType.DMA((2, 9)),
            pltpu.SemaphoreType.DMA((2, 9)),
        ],
        compiler_params=pltpu.CompilerParams(
            collective_id=0, has_side_effects=True, vmem_limit_bytes=52 << 20
        ),
    )(rhs, perm_h, perm_v, prolong, blk_slot, recv_slot.T, coarse_cols, coarse_off, coarse_diag)


def solution(mesh):
    placed = (
        P("sx", "sy", None),
        P("sx", "sy", None),
        P("sx", "sy", None),
        P(None, "sx", "sy", None),
        P(None, "sx", "sy"),
        P(None, ("sx", "sy")),
        P(None, ("sx", "sy")),
        P(None, ("sx", "sy")),
        P(None, ("sx", "sy")),
    )
    return jax.shard_map(
        shards, mesh=mesh, in_specs=placed, out_specs=P("sx", "sy", None), check_vma=False
    )
```

time: 823 us -> 160 us (0.19); the launches traced: 812 us -> 157 us
  matrix products: 309 us -> 0 us
  starting transfers between devices: 285 us -> 0 us
  Pallas kernels: 0 us -> 153 us
  waiting for transfers between devices: 105 us -> 0 us
  other arithmetic: 90.5 us -> 0 us
  local copies, waits for them, and re-layouts: 20.3 us -> 4.59 us
    dot_general x16 -> x0, matrix products: 309 us -> none  [the longest x8 286 us: shards(): jnp.einsum('oga,oa->g', coupling, whole, precision=highest, preferred_ele...]
    ppermute x92 -> x0, starting transfers between devices: 285 us -> none  [the longest x46 210 us: with_halo(): lax.ppermute(tail, axis, [(i, (i + 1) % count) for i in range(ends)])]
    pallas_call x0 -> x1, Pallas kernels: none -> 153 us  [shards(): pl.pallas_call(kernel, out_shape=jax.ShapeDtypeStruct(rhs.shape, f32), in...]
    ppermute x92 -> x0, waiting for transfers between devices: 105 us -> none  [the longest x46 86.3 us: with_halo(): lax.ppermute(head, axis, [((i + 1) % count, i) for i in range(ends)])]
    add x19 -> x0, other arithmetic: 57.1 us -> none  [the longest x1 31.1 us: shards(): coupling = coupling + coarse_off[term][None, :, None] * hits]
    mul x6 -> x0, local copies, waits for them, and re-layouts: 13.9 us -> none  [the longest x4 9.3 us: shards(): shaped * values[..., None]]
    sub x2 -> x0, other arithmetic: 11.8 us -> none  [shards(): resid = rhs - apply_op(pressure)]
    reduce_sum x4 -> x0, other arithmetic: 11 us -> none  [the longest x2 6.03 us: shards(): jnp.sum(shaped * values[..., None], axis=0)]
  transfers between devices with their start and end apart: 92 -> 0, of which waited for: 41 -> 0; matrix products, arithmetic and copies ran while one was open for 5% -> 0% of each run, Pallas kernels for 0% -> 0%
where the time goes in v1:
time: 160 us; the launch traced here: 157 us
  Pallas kernels  153 us (96%)
  local copies, waits for them, and re-layouts  4.59 us (3%)
    pallas_call x1, Pallas kernels, shards(): pl.pallas_call(kernel, out_shape=jax.ShapeDtypeStruct(rhs.shape, f32), in...  153 us
    unnamed x11, local copies, waits for them, and re-layouts  4.59 us

profile of v1, /device:TPU:7, one launch (start us, length us, event | category | flops | bytes accessed | tf_op | source)
XLA Modules:
  0.0 157.4 jit_solution(7874971888824882666)
XLA Ops:
  0.0 0.0 copy-start
  0.0 0.8 copy-done
  0.8 0.0 copy-start.1
  0.8 0.8 copy-done.1
  1.5 0.0 copy-start.2
  1.5 0.7 copy-done.2
  2.2 0.0 copy-start.3
  2.2 0.7 copy-done.3
  2.9 0.0 copy-start.4
  2.9 0.7 copy-done.4
  3.6 152.8 %shard_map.91 = f32[16,32,512]{2,1,0:T(8,128)S(1)} custom-call(f32[16,32,512]{2,1,0:T(8,128)} %rhs_h.1, f32[16,32,512]{2,1,0:T(8,128)} %ph_h.1, f32[16,32,512]{2,1,0:T(8,128)} %pv_h.1, f32[2,16,32,512]{3,2,1,0:T(8,128)} %pr_h.1, s32[2,16,128]{2,1,0:T(8,128)S(1)} %copy-done.2, s32[1,2304]{1,0:T(1,128)S(1)} %bitcast.1, s32[8,1024]{1,0:T(8,128)S(1)} %copy-done, ...), custom_call_target="tpu_custom_call" | custom-call | tf_op jit(solution)/shard_map/pallas_call | solution.py:404
  156.4 1.0 copy.11
Async XLA Ops:
  0.0 0.8 copy-start
  0.8 0.8 copy-start.1
  1.5 0.7 copy-start.2
  2.2 0.7 copy-start.3
  2.9 0.7 copy-start.4

commit v2 on v1

v2 whole, which is shorter than its diff:
```python
import functools

import jax
import jax.numpy as jnp
from jax import lax
from jax.experimental import pallas as pl
from jax.experimental.pallas import tpu as pltpu
from jax.sharding import PartitionSpec as P

CYCLES = 2
CJ = 4

storage_coef = 0.01
cheb_low = 0.25
cheb_high = 2.0
omega = 0.8

THETA = 0.5 * (cheb_high + cheb_low)
DELTA = 0.5 * (cheb_high - cheb_low)
SIGMA = THETA / DELTA
RHO0 = 1.0 / SIGMA
RHO1 = 1.0 / (2.0 * SIGMA - RHO0)
ALPHA = RHO1 * RHO0
BETA = 2.0 * RHO1 / DELTA

W = 3
T = 8
NX, NY, NZ = 16, 32, 512
TILES = (NY + 2 * T) // 8
MESH = pl.DeviceIdType.MESH
AROUND = (0, 1, 2, 3, 5, 6, 7, 8)
NEAR = tuple((dx, dy) for dx in range(-2, 3) for dy in range(-2, 3) if (dx, dy) != (0, 0))
f32 = jnp.float32
bf16 = jnp.bfloat16


def neighbour(dx, dy):
    x = lax.axis_index("sx") + dx
    y = lax.axis_index("sy") + dy
    there = (x >= 0) & (x < lax.axis_size("sx")) & (y >= 0) & (y < lax.axis_size("sy"))
    return x, y, there


def inverse(value):
    guess = pl.reciprocal(value, approx=True)
    return guess * (2.0 - value * guess)


def harmonic(left, right):
    total = left + right
    return 2.0 * left * right * inverse(jnp.where(total == 0.0, 1.0, total))


def pick(row, at):
    return jnp.take_along_axis(
        jnp.broadcast_to(row, at.shape), at & 127, axis=1, mode="promise_in_bounds"
    )


def pick_from(table_rows, at):
    high = at >> 7
    got = jnp.zeros(at.shape, f32)
    for r, row in enumerate(table_rows):
        got = jnp.where(high == r, pick(row(), at), got)
    return got


def kernel(
    rhs_h, ph_h, pv_h, pr_h, slot_h, recv_h, cols_h, off_h, diag_h, out_h,
    RHS, PH, PV, TE, TN, TU, INV, P0, P1, P2, PR, PKS, RKS, PKP, RKP, RKC,
    WH, WL, HOT, LHOT, AB, SLOT, LT, VT, RIDX, INVN, DIAN, MSG, ENT,
    OUT, ARR, RATN, TAB, T25, LIST, Y, BASE,
    slot_r, recv_r, cols_r, off_r, diag_r,
    in_sem, fsend, frecv, psend, precv, csend, crecv, wsend, wrecv,
):
    sub = lax.broadcasted_iota(jnp.int32, (8, 128), 0)
    lane = lax.broadcasted_iota(jnp.int32, (8, 128), 1)
    sub512 = lax.broadcasted_iota(jnp.int32, (8, NZ), 0)
    lane512 = lax.broadcasted_iota(jnp.int32, (8, NZ), 1)

    def rows(j):
        return slice(8 * j, 8 * j + 8)

    inner = pl.ds(T, NY)
    center = (pl.ds(W, NX), inner, slice(None))
    loads = [
        pltpu.make_async_copy(src, dst, in_sem.at[n])
        for n, (src, dst) in enumerate(
            [(ph_h, PH.at[center]), (pv_h, PV.at[center]), (rhs_h, RHS.at[center]),
             (slot_h, slot_r), (recv_h, recv_r), (cols_h, cols_r), (off_h, off_r), (diag_h, diag_r),
             (pr_h, PR)]
        )
    ]
    for load in loads:
        load.start()

    bar = pltpu.get_barrier_semaphore()
    for dx, dy in NEAR:
        x, y, there = neighbour(dx, dy)

        @pl.when(there)
        def _():
            pl.semaphore_signal(bar, inc=1, device_id=(x, y), device_id_type=MESH)

    def clear(view):
        def one(i, carry):
            view[i] = jnp.zeros(view.shape[1:], f32)
            return carry

        lax.fori_loop(0, view.shape[0], one, 0)

    for array in (PH, PV, RHS, P0, P2):
        for dx, strip in ((-1, pl.ds(0, W)), (1, pl.ds(W + NX, W))):
            _, _, there = neighbour(dx, 0)

            @pl.when(jnp.logical_not(there))
            def _():
                clear(array.at[strip])

    for i in (0, 2 * W + NX - 1):
        for j in (0, TILES - 1):
            PH[i, rows(j), :] = jnp.zeros((8, NZ), f32)
    for side, dy in ((0, -1), (1, 1)):
        _, _, there = neighbour(0, dy)

        @pl.when(jnp.logical_not(there))
        def _():
            clear(RKS.at[side])
            clear(P0.at[:, pl.ds(0 if side == 0 else T + NY, T), :])
            clear(P2.at[:, pl.ds(0 if side == 0 else T + NY, T), :])

    for dx, strip in ((-1, pl.ds(0, 2)), (1, pl.ds(NX + 2, 2))):
        _, _, there = neighbour(dx, 0)

        @pl.when(jnp.logical_not(there))
        def _():
            clear(RKS.at[0, strip])
            clear(RKS.at[1, strip])

    for load in loads[:3]:
        load.wait()

    def pack_first(x, carry):
        i = x + W
        a, b, c = PH[i, rows(1), :], PV[i, rows(1), :], RHS[i, rows(1), :]
        PKS[0, x] = jnp.where(sub512 < 3, a, jnp.where(sub512 < 5, pltpu.roll(b, 3, 0), pltpu.roll(c, 5, 0)))
        a, b, c = PH[i, rows(4), :], PV[i, rows(4), :], RHS[i, rows(4), :]
        PKS[1, x] = jnp.where(sub512 >= 5, a, jnp.where(sub512 >= 3, pltpu.roll(b, 5, 0), pltpu.roll(c, 3, 0)))
        return carry

    lax.fori_loop(0, NX, pack_first, 0)

    peers = sum(neighbour(dx, dy)[2].astype(jnp.int32) for dx, dy in NEAR)
    pl.semaphore_wait(bar, peers)

    def go(copies):
        for there, copy, _ in copies:
            @pl.when(there)
            def _():
                copy.start()

    def land(copies):
        for there, copy, arrive in copies:
            @pl.when(there)
            def _():
                arrive.wait_recv()
                copy.wait_send()

    def moved(to, src, there_dst, here_dst, send, recv_there, recv_here):
        x, y, there = neighbour(*to)
        copy = pltpu.make_async_remote_copy(
            src, there_dst, send, recv_there, device_id=(x, y), device_id_type=MESH
        )
        arrive = pltpu.make_async_remote_copy(
            here_dst, here_dst, send, recv_here, device_id=(x, y), device_id_type=MESH
        )
        return there, copy, arrive

    def x_strips(field, src, base, width, send, recv):
        out = []
        for dx in (-1, 1):
            if dx < 0:
                take, put, get = base, W + NX, W - width
            else:
                take, put, get = base + NX - width, W - width, W + NX
            pick_y = inner if base else slice(None)
            out.append(moved(
                (dx, 0), src.at[pl.ds(take, width), pick_y, :], field.at[pl.ds(put, width), inner, :],
                field.at[pl.ds(get, width), inner, :],
                send.at[(dx + 1) // 2], recv.at[(1 - dx) // 2], recv.at[(dx + 1) // 2],
            ))
        return out

    first = []
    for dy in (-1, 1):
        side = (dy + 1) // 2
        for dx in (0, -1, 1):
            src = {0: pl.ds(0, NX), -1: pl.ds(0, 2), 1: pl.ds(NX - 2, 2)}[dx]
            put = {0: pl.ds(2, NX), -1: pl.ds(NX + 2, 2), 1: pl.ds(0, 2)}[dx]
            get = {0: pl.ds(2, NX), -1: pl.ds(0, 2), 1: pl.ds(NX + 2, 2)}[dx]
            first.append(moved(
                (dx, dy), PKS.at[side, src], RKS.at[1 - side, put], RKS.at[side, get],
                fsend.at[3, dx + 1 + 3 * side], frecv.at[3, 1 - dx + 3 * (1 - side)],
                frecv.at[3, dx + 1 + 3 * side],
            ))
    for n, (field, src, width) in enumerate(((PH, ph_h, 3), (PV, pv_h, 2), (RHS, rhs_h, 2))):
        first += x_strips(field, src, 0, width, fsend.at[n], frecv.at[n])
    go(first)

    for load in loads[3:]:
        load.wait()
    for k in range(2):
        for x8 in range(2):
            raw = slot_r[k, 8 * x8:8 * x8 + 8, :]
            order = (((lane >> 5) << 3) + (lane & 7)) * 4 + ((lane >> 3) & 3)
            SLOT[pl.ds(16 * k + 8 * x8, 8), :] = jnp.take_along_axis(
                raw, order, axis=1, mode="promise_in_bounds"
            )
    RIDX[...] = jnp.full_like(RIDX, 1024)
    for r in range(18):
        RIDX[r:r + 1, :] = recv_r[0:1, r * 128:(r + 1) * 128]
    low = lax.broadcasted_iota(jnp.int32, (128, 128), 0)
    cnum = lane.astype(f32) + 1.0
    for o in range(9):
        total = jnp.zeros((8, 128), f32)
        for h in range(2):
            ids = RIDX[2 * o + h:2 * o + h + 1, :]
            a = jnp.where(jnp.broadcast_to(ids >> 7, (8, 128)) == sub, cnum + 128.0 * h, 0.0)
            b = (jnp.broadcast_to(ids & 127, (128, 128)) == low).astype(f32)
            total = total + lax.dot_general(
                a.astype(bf16), b.astype(bf16), (((1,), (1,)), ((), ())),
                preferred_element_type=f32,
            )
        INVN[4, o] = (total + 0.5).astype(jnp.int32) - 1
    for m in range(8):
        DIAN[4, m:m + 1, :] = diag_r[0:1, m * 128:(m + 1) * 128]
    DIAN[4] = 1.0 / DIAN[4]
    for o in range(9):
        for h in range(2):
            at = jnp.broadcast_to(RIDX[2 * o + h:2 * o + h + 1, :], (8, 128))
            at = jnp.where(at == 1024, 0, at)
            cols = jnp.zeros((8, 128), f32)
            offs = jnp.zeros((8, 128), f32)
            for m in range(8):
                piece = slice(128 * m, 128 * m + 128)
                hit = (at >> 7) == m
                cols = jnp.where(hit, pick(cols_r[:, piece].astype(f32), at), cols)
                offs = jnp.where(hit, pick(off_r[:, piece], at), offs)
            MSG[o, h, 0:8, :] = cols
            MSG[o, h, 8:16, :] = offs
            MSG[o, h, 16:24, :] = at.astype(f32)
    ENT[4] = MSG[4]

    def around(src, dst, send, recv):
        out = []
        for o in AROUND:
            out.append(moved(
                (o // 3 - 1, o % 3 - 1), src(o), dst.at[8 - o], dst.at[o],
                send.at[o], recv.at[8 - o], recv.at[o],
            ))
        return out

    tables = []
    for o in AROUND:
        to = (o // 3 - 1, o % 3 - 1)
        tables.append(moved(to, INVN.at[4], INVN.at[8 - o], INVN.at[o], wsend.at[0, o], wrecv.at[0, 8 - o], wrecv.at[0, o]))
        tables.append(moved(to, DIAN.at[4], DIAN.at[8 - o], DIAN.at[o], wsend.at[1, o], wrecv.at[1, 8 - o], wrecv.at[1, o]))
    tables += around(lambda o: MSG.at[o], ENT, wsend.at[2], wrecv.at[2])
    go(tables)

    LT[...] = jnp.zeros_like(LT)
    LT[0:32, :] = SLOT[...] & 127
    LT[...] = LT[...].T
    lane_all = lax.broadcasted_iota(jnp.int32, (128, 128), 1)
    row24 = lax.broadcasted_iota(jnp.int32, (24, 128), 0)
    for kx in range(32):
        line = jnp.broadcast_to(SLOT[kx:kx + 1, :] >> 7, (24, 128))
        HOT[:, kx * 128:(kx + 1) * 128] = (line == row24).astype(f32)
        LHOT[kx * 128:(kx + 1) * 128, :] = (
            jnp.broadcast_to(LT[:, kx:kx + 1], (128, 128)) == lane_all
        ).astype(f32).astype(bf16)
    AB[...] = jnp.zeros_like(AB)

    def edge_x(i, tiles):
        for j in tiles:
            TE[i, rows(j), :] = harmonic(PH[i, rows(j), :], PH[i + 1, rows(j), :])

    def edge_yz(i, new, done):
        for j in new:
            ctr = PH[i, rows(j), :]
            if j < TILES - 1:
                up = PH[i, 8 * j + 1:8 * j + 9, :]
            else:
                up = pltpu.roll(ctr, 7, 0)
            TN[i, rows(j), :] = harmonic(ctr, up)
            pv = PV[i, rows(j), :]
            TU[i, rows(j), :] = jnp.where(
                lane512 == NZ - 1, 0.0, harmonic(pv, pltpu.roll(pv, NZ - 1, 1))
            )
        for j in done:
            tn = TN[i, rows(j), :]
            down = TN[i, 8 * j - 1:8 * j + 7, :] if j > 0 else pltpu.roll(tn, 1, 0)
            tu = TU[i, rows(j), :]
            total = storage_coef + TE[i, rows(j), :] + TE[i - 1, rows(j), :] + tn + down + tu + pltpu.roll(tu, 1, 1)
            INV[i, rows(j), :] = inverse(total)

    def loop(lo, hi, fn):
        def body(i, carry):
            fn(i)
            return carry

        lax.fori_loop(lo, hi, body, 0)

    every = tuple(range(TILES))
    loop(W, W + NX - 1, lambda i: edge_x(i, (1, 2, 3, 4)))
    loop(W + 1, W + NX - 1, lambda i: edge_yz(i, (1, 2, 3), (2, 3)))

    land(first)

    def unpack_first(i):
        got = RKS[0, i - 1]
        PH[i, rows(0), :] = jnp.where(sub512 >= 5, got, 0.0)
        PV[i, rows(0), :] = jnp.where(sub512 >= 6, pltpu.roll(got, 3, 0), 0.0)
        RHS[i, rows(0), :] = jnp.where(sub512 >= 6, pltpu.roll(got, 5, 0), 0.0)
        got = RKS[1, i - 1]
        PH[i, rows(5), :] = jnp.where(sub512 < 3, got, 0.0)
        PV[i, rows(5), :] = jnp.where(sub512 < 2, pltpu.roll(got, 5, 0), 0.0)
        RHS[i, rows(5), :] = jnp.where(sub512 < 2, pltpu.roll(got, 3, 0), 0.0)

    loop(1, NX + 5, unpack_first)
    for lo, hi in ((0, W), (W + NX - 1, 2 * W + NX - 1)):
        loop(lo, hi, lambda i: edge_x(i, every))
    loop(W, W + NX - 1, lambda i: edge_x(i, (0, 5)))
    for lo, hi in ((1, W + 1), (W + NX - 1, 2 * W + NX - 1)):
        loop(lo, hi, lambda i: edge_yz(i, every, every))
    loop(W + 1, W + NX - 1, lambda i: edge_yz(i, (0, 4, 5), (0, 1, 4, 5)))

    def residual(field, i, j):
        ctr = field[i, rows(j), :]
        acc = RHS[i, rows(j), :] - storage_coef * ctr
        acc = acc + TE[i, rows(j), :] * (field[i + 1, rows(j), :] - ctr)
        acc = acc + TE[i - 1, rows(j), :] * (field[i - 1, rows(j), :] - ctr)
        fz = TU[i, rows(j), :] * (pltpu.roll(ctr, NZ - 1, 1) - ctr)
        acc = acc + fz - pltpu.roll(fz, 1, 1)
        if j < TILES - 1:
            up = field[i, 8 * j + 1:8 * j + 9, :]
        else:
            up = pltpu.roll(ctr, 7, 0)
        fn = TN[i, rows(j), :] * (up - ctr)
        if j > 0:
            fs = TN[i, 8 * j - 1:8 * j + 7, :] * (ctr - field[i, 8 * j - 1:8 * j + 7, :])
        else:
            fs = pltpu.roll(fn, 1, 0)
        return ctr, acc + fn - fs

    def sweep(extent, update):
        tiles = range(TILES) if extent > 0 else range(1, TILES - 1)

        def body(i):
            for j in tiles:
                update(i, j)

        loop(W - extent, W + NX + extent, body)

    def start_from_zero(i, j):
        P1[i, rows(j), :] = (1.0 / THETA) * INV[i, rows(j), :] * RHS[i, rows(j), :]

    def sweep_a(field, i, j):
        ctr, res = residual(field, i, j)
        P1[i, rows(j), :] = ctr + (1.0 / THETA) * INV[i, rows(j), :] * res

    def sweep_b_first(i, j):
        ctr, res = residual(P1, i, j)
        P0[i, rows(j), :] = (1.0 + ALPHA) * ctr + BETA * INV[i, rows(j), :] * res

    def sweep_b(old, new, i, j):
        ctr, res = residual(P1, i, j)
        new[i, rows(j), :] = (1.0 + ALPHA) * ctr - ALPHA * old[i, rows(j), :] + BETA * INV[i, rows(j), :] * res

    def exchange_pressure(field, width, slot):
        per = 8 // (2 if width == 2 else 4)
        span = 8 // per
        tiles = NX // per

        def pack(g):
            a = b = None
            for m in range(per):
                i = W + g * per + m
                one = field[i, rows(1), :]
                two = field[i, rows(4), :]
                one = one if m == 0 else pltpu.roll(one, m * span, 0)
                two = two if (m + 1) * span == 8 else pltpu.roll(two, (m + 1) * span, 0)
                a = one if a is None else jnp.where(sub512 >= m * span, one, a)
                b = two if b is None else jnp.where(sub512 >= m * span, two, b)
            PKP[0, g] = a
            PKP[1, g] = b

        loop(0, tiles, pack)
        step = x_strips(field, field, W, width, psend.at[slot, 0], precv.at[slot, 0])
        for dy in (-1, 1):
            side = (dy + 1) // 2
            step.append(moved(
                (0, dy), PKP.at[side, pl.ds(0, tiles)], RKP.at[slot, 1 - side, pl.ds(0, tiles)],
                RKP.at[slot, side, pl.ds(0, tiles)],
                psend.at[slot, 1, side], precv.at[slot, 1, 1 - side], precv.at[slot, 1, side],
            ))
            for dx in (-1, 1):
                far = (dx + 1) // 2
                step.append(moved(
                    (dx, dy), PKP.at[side, 0 if dx < 0 else tiles - 1], RKC.at[slot, 1 - side, 1 - far],
                    RKC.at[slot, side, far],
                    psend.at[slot, 2 + side, far], precv.at[slot, 2 + 1 - side, 1 - far], precv.at[slot, 2 + side, far],
                ))
        go(step)
        land(step)

        def place(side, tile, m, i):
            if side == 0:
                turn = (8 - span - m * span) % 8
            else:
                turn = (-m * span) % 8
            tile = pltpu.roll(tile, turn, 0) if turn else tile
            field[i, rows(0 if side == 0 else 5), :] = tile

        for side, dy in ((0, -1), (1, 1)):
            _, _, there = neighbour(0, dy)

            @pl.when(there)
            def _():
                def body(g):
                    tile = RKP[slot, side, g]
                    for m in range(per):
                        place(side, tile, m, W + g * per + m)

                loop(0, tiles, body)

            for far, dx in ((0, -1), (1, 1)):
                _, _, there = neighbour(dx, dy)

                @pl.when(there)
                def _():
                    tile = RKC[slot, side, far]
                    for depth in range(width - 1):
                        if dx < 0:
                            place(side, tile, per - 1 - depth, W - 1 - depth)
                        else:
                            place(side, tile, depth, W + NX + depth)

    def restrict(field, i):
        x = i - W
        for j in range(1, TILES - 1):
            _, res = residual(field, i, j)
            t = j - 1
            for k in range(2):
                scaled = PR[k, x, 8 * t:8 * t + 8, :] * res
                for h in range(2):
                    both = jnp.concatenate(
                        [scaled[:, 256 * h:256 * h + 128], scaled[:, 256 * h + 128:256 * h + 256]], axis=0
                    )
                    high = both.astype(bf16)
                    at = pl.multiple_of((16 * k + x) * 128 + (t * 4 + 2 * h) * 8, 16)
                    WH[pl.ds(at, 16), :] = high
                    WL[pl.ds(at, 16), :] = (both - high.astype(f32)).astype(bf16)

    def wide(src, dst, parity, lists):
        out = []
        for n, (dx, dy) in enumerate(NEAR):
            if lists:
                def rect(ax, ay):
                    x0, x1 = max(-1, ax - 1) + 1, min(1, ax + 1) + 2
                    y0, y1 = max(-1, ay - 1) + 1, min(1, ay + 1) + 2
                    return pl.ds(x0, x1 - x0), pl.ds(y0, y1 - y0)
                give, take = rect(dx, dy), rect(-dx, -dy)
                piece, put, get = src.at[give], dst.at[(2 - dx, 2 - dy) + give], dst.at[(2 + dx, 2 + dy) + take]
            else:
                piece, put, get = src, dst.at[2 - dx, 2 - dy], dst.at[2 + dx, 2 + dy]
            out.append(moved(
                (dx, dy), piece, put, get, wsend.at[3 + parity, n], wrecv.at[3 + parity, 23 - n],
                wrecv.at[3 + parity, n],
            ))
        return out

    def jacobi(table):
        for m in range(8):
            at = cols_r[:, 128 * m:128 * m + 128]
            got = pick_from([lambda r=r: table[r // 8, r % 8:r % 8 + 1, :] for r in range(72)], at)
            coupled = jnp.sum(got * off_r[:, 128 * m:128 * m + 128], axis=0, keepdims=True)
            mine = table[4, m:m + 1, :]
            Y[m:m + 1, :] = mine + omega * (RATN[4, m:m + 1, :] - mine - coupled)

    def coarse(field, cycle):
        ones = jnp.ones((16, 128), bf16)
        along = (((1,), (1,)), ((), ()))
        sums = lax.dot_general(ones, WH[...], along, preferred_element_type=f32)
        sums = sums + lax.dot_general(ones, WL[...], along, preferred_element_type=f32)
        for r in range(3):
            if r < 2:
                part = HOT[8 * r:8 * r + 8, :] * sums[0:8]
            else:
                part = HOT[16:24, :] * sums[0:8]
            if r % 2 == 0:
                kept = part
            if r == 1:
                both = jnp.concatenate([kept, part], axis=0)
                high = both.astype(bf16)
                AB[0:16, :] = high
                AB[32:48, :] = (both - high.astype(f32)).astype(bf16)
            if r == 2:
                both = jnp.concatenate([part, jnp.zeros_like(part)], axis=0)
                high = both.astype(bf16)
                AB[16:32, :] = high
                AB[48:64, :] = (both - high.astype(f32)).astype(bf16)
        listed = jnp.dot(AB[...], LHOT[...], preferred_element_type=f32)
        listed = listed[0:32] + listed[32:64]
        for r in range(18):
            o, h = r // 2, r % 2
            OUT[o // 3, o % 3, h:h + 1, :] = listed[r:r + 1, :]
        step = wide(OUT, ARR, 0, True)
        go(step)
        ARR[2, 2] = OUT[...]
        if cycle == 0:
            land(tables)
        land(step)
        for p in range(9):
            total = jnp.zeros((8, 128), f32)
            for o in range(9):
                at = INVN[p, o]
                sx, sy = p // 3 + o // 3, p % 3 + o % 3
                other = 8 - o
                for h in range(2):
                    got = pick(ARR[sx, sy, other // 3, other % 3, h:h + 1, :], at)
                    total = total + jnp.where((at >> 7) == h, got, 0.0)
            ratio = total * DIAN[p]
            RATN[p] = ratio
            TAB[0, p] = omega * ratio
        jacobi(TAB.at[0])
        for s in range(1, CJ - 1):
            table = TAB.at[s % 2]
            step = around(lambda o: Y, table, csend.at[s % 2], crecv.at[s % 2])
            go(step)
            table[4] = Y[...]
            land(step)
            jacobi(table)
        step = wide(Y, T25, 1, False)
        go(step)
        T25[2, 2] = Y[...]
        land(step)
        for o in range(9):
            BASE[o] = (1.0 - omega) * T25[1 + o // 3, 1 + o % 3] + omega * RATN[o]

        for o in range(9):
            ox, oy = o // 3, o % 3
            for h in range(2):
                at = ENT[o, h, 16:24, :].astype(jnp.int32)
                base = pick_from([lambda r=r: BASE[o, r:r + 1, :] for r in range(8)], at)
                at = ENT[o, h, 0:8, :].astype(jnp.int32)
                got = pick_from(
                    [lambda r=r: T25[ox + r // 24, oy + (r // 8) % 3, r % 8:r % 8 + 1, :] for r in range(72)], at
                )
                coupled = jnp.sum(got * ENT[o, h, 8:16, :], axis=0, keepdims=True)
                LIST[o, h:h + 1, :] = base[0:1, :] - omega * coupled

        for r4 in range(4):
            VT[8 * r4:8 * r4 + 8, :] = pick_from(
                [lambda r=r: LIST[r // 2, r % 2:r % 2 + 1, :] for r in range(18)], SLOT[8 * r4:8 * r4 + 8, :]
            )
        VT[...] = VT[...].T

        def correct(x):
            for t in range(4):
                total = field[x + W, T + 8 * t:T + 8 * t + 8, :]
                for k in range(2):
                    which = jnp.full((8, 128), 16 * k, jnp.int32) + x
                    spread = []
                    for zb in range(4):
                        b0 = (t * 4 + zb) * 8
                        spread.append(
                            jnp.take_along_axis(VT[b0:b0 + 8, :], which, axis=1, mode="promise_in_bounds")
                        )
                    total = total + PR[k, x, 8 * t:8 * t + 8, :] * jnp.concatenate(spread, axis=1)
                field[x + W, T + 8 * t:T + 8 * t + 8, :] = total

        loop(0, NX, correct)

    VT[...] = jnp.zeros_like(VT)
    for cycle in range(CYCLES):
        field = (P0, P2)[cycle]
        if cycle == 0:
            sweep(2, start_from_zero)
            sweep(1, sweep_b_first)
        else:
            exchange_pressure(field, 3, 1)
            sweep(2, functools.partial(sweep_a, field))
            sweep(1, functools.partial(sweep_b, field, field))
        loop(W, W + NX, functools.partial(restrict, field))
        coarse(field, cycle)
        exchange_pressure(field, 2, 0)
        sweep(1, functools.partial(sweep_a, field))
        sweep(0, functools.partial(sweep_b, field, P2))
    back = pltpu.make_async_copy(P2.at[center], out_h, in_sem.at[0])
    back.start()
    back.wait()


def shards(rhs, perm_h, perm_v, prolong, blk_slot, recv_slot, coarse_cols, coarse_off, coarse_diag):
    padded = pltpu.VMEM((2 * W + NX, 2 * T + NY, NZ), f32)
    hbm = pl.BlockSpec(memory_space=pltpu.HBM)
    i32 = jnp.int32
    return pl.pallas_call(
        kernel,
        out_shape=jax.ShapeDtypeStruct(rhs.shape, f32),
        in_specs=[hbm] * 9,
        out_specs=hbm,
        scratch_shapes=[padded] * 10
        + [
            pltpu.VMEM((2, NX, NY, NZ), f32),
            pltpu.VMEM((2, NX, 8, NZ), f32),
            pltpu.VMEM((2, NX + 4, 8, NZ), f32),
            pltpu.VMEM((2, 8, 8, NZ), f32),
            pltpu.VMEM((2, 2, 8, 8, NZ), f32),
            pltpu.VMEM((2, 2, 2, 8, NZ), f32),
            pltpu.VMEM((4096, 128), bf16),
            pltpu.VMEM((4096, 128), bf16),
            pltpu.VMEM((24, 4096), f32),
            pltpu.VMEM((4096, 128), bf16),
            pltpu.VMEM((64, 4096), bf16),
            pltpu.VMEM((32, 128), i32),
            pltpu.VMEM((128, 128), i32),
            pltpu.VMEM((128, 128), f32),
            pltpu.VMEM((24, 128), i32),
            pltpu.VMEM((9, 9, 8, 128), i32),
            pltpu.VMEM((9, 8, 128), f32),
            pltpu.VMEM((9, 2, 24, 128), f32),
            pltpu.VMEM((9, 2, 24, 128), f32),
            pltpu.VMEM((3, 3, 2, 128), f32),
            pltpu.VMEM((5, 5, 3, 3, 2, 128), f32),
            pltpu.VMEM((9, 8, 128), f32),
            pltpu.VMEM((2, 9, 8, 128), f32),
            pltpu.VMEM((5, 5, 8, 128), f32),
            pltpu.VMEM((9, 2, 128), f32),
            pltpu.VMEM((8, 128), f32),
            pltpu.VMEM((9, 8, 128), f32),
            pltpu.VMEM((2, NX, 128), i32),
            pltpu.VMEM((1, 2304), i32),
            pltpu.VMEM((8, 1024), i32),
            pltpu.VMEM((8, 1024), f32),
            pltpu.VMEM((1, 1024), f32),
            pltpu.SemaphoreType.DMA((9,)),
            pltpu.SemaphoreType.DMA((4, 6)),
            pltpu.SemaphoreType.DMA((4, 6)),
            pltpu.SemaphoreType.DMA((2, 4, 2)),
            pltpu.SemaphoreType.DMA((2, 4, 2)),
            pltpu.SemaphoreType.DMA((2, 9)),
            pltpu.SemaphoreType.DMA((2, 9)),
            pltpu.SemaphoreType.DMA((5, 24)),
            pltpu.SemaphoreType.DMA((5, 24)),
        ],
        compiler_params=pltpu.CompilerParams(
            collective_id=0, has_side_effects=True, vmem_limit_bytes=52 << 20
        ),
    )(rhs, perm_h, perm_v, prolong, blk_slot, recv_slot.T, coarse_cols, coarse_off, coarse_diag)


def solution(mesh):
    placed = (
        P("sx", "sy", None),
        P("sx", "sy", None),
        P("sx", "sy", None),
        P(None, "sx", "sy", None),
        P(None, "sx", "sy"),
        P(None, ("sx", "sy")),
        P(None, ("sx", "sy")),
        P(None, ("sx", "sy")),
        P(None, ("sx", "sy")),
    )
    return jax.shard_map(
        shards, mesh=mesh, in_specs=placed, out_specs=P("sx", "sy", None), check_vma=False
    )
```

time: 160 us -> 121 us (0.76); the launches traced: 157 us -> 121 us
  Pallas kernels: 153 us -> 117 us
    pallas_call x1, Pallas kernels: 153 us -> 117 us  [shards(): pl.pallas_call(kernel, out_shape=jax.ShapeDtypeStruct(rhs.shape, f32), in...]
where the time goes in v2:
time: 121 us
  Pallas kernels  117 us (97%)
  local copies, waits for them, and re-layouts  4.59 us (4%)
    pallas_call x1, Pallas kernels, shards(): pl.pallas_call(kernel, out_shape=jax.ShapeDtypeStruct(rhs.shape, f32), in...  117 us
    unnamed x11, local copies, waits for them, and re-layouts  4.59 us

profile of v2, /device:TPU:7, one launch (start us, length us, event | category | flops | bytes accessed | tf_op | source)
XLA Modules:
  0.0 121.1 jit_solution(5606270646466924027)
XLA Ops:
  0.0 0.0 copy-start
  0.0 0.8 copy-done
  0.8 0.0 copy-start.1
  0.8 0.8 copy-done.1
  1.5 0.0 copy-start.2
  1.5 0.7 copy-done.2
  2.2 0.0 copy-start.3
  2.2 0.7 copy-done.3
  2.9 0.0 copy-start.4
  2.9 0.7 copy-done.4
  3.6 116.5 %shard_map.91 = f32[16,32,512]{2,1,0:T(8,128)S(1)} custom-call(f32[16,32,512]{2,1,0:T(8,128)} %rhs_h.1, f32[16,32,512]{2,1,0:T(8,128)} %ph_h.1, f32[16,32,512]{2,1,0:T(8,128)} %pv_h.1, f32[2,16,32,512]{3,2,1,0:T(8,128)} %pr_h.1, s32[2,16,128]{2,1,0:T(8,128)S(1)} %copy-done.2, s32[1,2304]{1,0:T(1,128)S(1)} %bitcast.1, s32[8,1024]{1,0:T(8,128)S(1)} %copy-done, ...), custom_call_target="tpu_custom_call" | custom-call | tf_op jit(solution)/shard_map/pallas_call | solution.py:609
  120.1 1.0 copy.11
Async XLA Ops:
  0.0 0.8 copy-start
  0.8 0.8 copy-start.1
  1.5 0.7 copy-start.2
  2.2 0.7 copy-start.3
  2.9 0.7 copy-start.4

commit v3 on v2

--- a/solution.py
+++ b/solution.py
@@ -28,7 +28,7 @@
 NX, NY, NZ = 16, 32, 512
 TILES = (NY + 2 * T) // 8
 MESH = pl.DeviceIdType.MESH
-AROUND = (0, 1, 2, 3, 5, 6, 7, 8)
+AROUND = (0, 2, 6, 8, 3, 5, 1, 7)
 NEAR = tuple((dx, dy) for dx in range(-2, 3) for dy in range(-2, 3) if (dx, dy) != (0, 0))
 f32 = jnp.float32
 bf16 = jnp.bfloat16
@@ -95,19 +95,30 @@
         load.start()
 
     bar = pltpu.get_barrier_semaphore()
-    for dx, dy in NEAR:
-        x, y, there = neighbour(dx, dy)
+    for o in AROUND:
+        x, y, there = neighbour(o // 3 - 1, o % 3 - 1)
 
         @pl.when(there)
         def _():
             pl.semaphore_signal(bar, inc=1, device_id=(x, y), device_id_type=MESH)
 
+    def loop(lo, hi, fn):
+        pairs = (hi - lo) // 2
+
+        def body(n, carry):
+            fn(lo + 2 * n)
+            fn(lo + 2 * n + 1)
+            return carry
+
+        lax.fori_loop(0, pairs, body, 0)
+        if (hi - lo) % 2:
+            fn(hi - 1)
+
     def clear(view):
-        def one(i, carry):
+        def one(i):
             view[i] = jnp.zeros(view.shape[1:], f32)
-            return carry
-
-        lax.fori_loop(0, view.shape[0], one, 0)
+
+        loop(0, view.shape[0], one)
 
     for array in (PH, PV, RHS, P0, P2):
         for dx, strip in ((-1, pl.ds(0, W)), (1, pl.ds(W + NX, W))):
@@ -140,17 +151,16 @@
     for load in loads[:3]:
         load.wait()
 
-    def pack_first(x, carry):
+    def pack_first(x):
         i = x + W
         a, b, c = PH[i, rows(1), :], PV[i, rows(1), :], RHS[i, rows(1), :]
         PKS[0, x] = jnp.where(sub512 < 3, a, jnp.where(sub512 < 5, pltpu.roll(b, 3, 0), pltpu.roll(c, 5, 0)))
         a, b, c = PH[i, rows(4), :], PV[i, rows(4), :], RHS[i, rows(4), :]
         PKS[1, x] = jnp.where(sub512 >= 5, a, jnp.where(sub512 >= 3, pltpu.roll(b, 5, 0), pltpu.roll(c, 3, 0)))
-        return carry
-
-    lax.fori_loop(0, NX, pack_first, 0)
-
-    peers = sum(neighbour(dx, dy)[2].astype(jnp.int32) for dx, dy in NEAR)
+
+    loop(0, NX, pack_first)
+
+    peers = sum(neighbour(o // 3 - 1, o % 3 - 1)[2].astype(jnp.int32) for o in AROUND)
     pl.semaphore_wait(bar, peers)
 
     def go(copies):
@@ -304,13 +314,6 @@
             total = storage_coef + TE[i, rows(j), :] + TE[i - 1, rows(j), :] + tn + down + tu + pltpu.roll(tu, 1, 1)
             INV[i, rows(j), :] = inverse(total)
 
-    def loop(lo, hi, fn):
-        def body(i, carry):
-            fn(i)
-            return carry
-
-        lax.fori_loop(lo, hi, body, 0)
-
     every = tuple(range(TILES))
     loop(W, W + NX - 1, lambda i: edge_x(i, (1, 2, 3, 4)))
     loop(W + 1, W + NX - 1, lambda i: edge_yz(i, (1, 2, 3), (2, 3)))
@@ -335,49 +338,50 @@
         loop(lo, hi, lambda i: edge_yz(i, every, every))
     loop(W + 1, W + NX - 1, lambda i: edge_yz(i, (0, 4, 5), (0, 1, 4, 5)))
 
-    def residual(field, i, j):
-        ctr = field[i, rows(j), :]
-        acc = RHS[i, rows(j), :] - storage_coef * ctr
-        acc = acc + TE[i, rows(j), :] * (field[i + 1, rows(j), :] - ctr)
-        acc = acc + TE[i - 1, rows(j), :] * (field[i - 1, rows(j), :] - ctr)
-        fz = TU[i, rows(j), :] * (pltpu.roll(ctr, NZ - 1, 1) - ctr)
-        acc = acc + fz - pltpu.roll(fz, 1, 1)
-        if j < TILES - 1:
-            up = field[i, 8 * j + 1:8 * j + 9, :]
-        else:
+    def residuals(field, i, tiles):
+        before = None
+        for j in tiles:
+            ctr = field[i, rows(j), :]
+            acc = RHS[i, rows(j), :] - storage_coef * ctr
+            acc = acc + TE[i, rows(j), :] * (field[i + 1, rows(j), :] - ctr)
+            acc = acc + TE[i - 1, rows(j), :] * (field[i - 1, rows(j), :] - ctr)
+            fz = TU[i, rows(j), :] * (pltpu.roll(ctr, NZ - 1, 1) - ctr)
+            acc = acc + fz - pltpu.roll(fz, 1, 1)
             up = pltpu.roll(ctr, 7, 0)
-        fn = TN[i, rows(j), :] * (up - ctr)
-        if j > 0:
-            fs = TN[i, 8 * j - 1:8 * j + 7, :] * (ctr - field[i, 8 * j - 1:8 * j + 7, :])
-        else:
-            fs = pltpu.roll(fn, 1, 0)
-        return ctr, acc + fn - fs
+            if j < TILES - 1:
+                up = jnp.where(sub512 == 7, pltpu.roll(field[i, rows(j + 1), :], 7, 0), up)
+            fn = TN[i, rows(j), :] * (up - ctr)
+            turned = pltpu.roll(fn, 1, 0)
+            if before is not None:
+                fs = jnp.where(sub512 == 0, before, turned)
+            elif j > 0:
+                fs = TN[i, 8 * j - 1:8 * j + 7, :] * (ctr - field[i, 8 * j - 1:8 * j + 7, :])
+            else:
+                fs = turned
+            before = turned
+            yield j, ctr, acc + fn - fs
 
     def sweep(extent, update):
-        tiles = range(TILES) if extent > 0 else range(1, TILES - 1)
-
-        def body(i):
-            for j in tiles:
-                update(i, j)
-
-        loop(W - extent, W + NX + extent, body)
-
-    def start_from_zero(i, j):
-        P1[i, rows(j), :] = (1.0 / THETA) * INV[i, rows(j), :] * RHS[i, rows(j), :]
-
-    def sweep_a(field, i, j):
-        ctr, res = residual(field, i, j)
-        P1[i, rows(j), :] = ctr + (1.0 / THETA) * INV[i, rows(j), :] * res
-
-    def sweep_b_first(i, j):
-        ctr, res = residual(P1, i, j)
-        P0[i, rows(j), :] = (1.0 + ALPHA) * ctr + BETA * INV[i, rows(j), :] * res
-
-    def sweep_b(old, new, i, j):
-        ctr, res = residual(P1, i, j)
-        new[i, rows(j), :] = (1.0 + ALPHA) * ctr - ALPHA * old[i, rows(j), :] + BETA * INV[i, rows(j), :] * res
-
-    def exchange_pressure(field, width, slot):
+        tiles = tuple(range(TILES)) if extent > 0 else tuple(range(1, TILES - 1))
+        loop(W - extent, W + NX + extent, lambda i: update(i, tiles))
+
+    def start_from_zero(i, tiles):
+        for j in tiles:
+            P1[i, rows(j), :] = (1.0 / THETA) * INV[i, rows(j), :] * RHS[i, rows(j), :]
+
+    def sweep_a(field, i, tiles):
+        for j, ctr, res in residuals(field, i, tiles):
+            P1[i, rows(j), :] = ctr + (1.0 / THETA) * INV[i, rows(j), :] * res
+
+    def sweep_b_first(i, tiles):
+        for j, ctr, res in residuals(P1, i, tiles):
+            P0[i, rows(j), :] = (1.0 + ALPHA) * ctr + BETA * INV[i, rows(j), :] * res
+
+    def sweep_b(old, new, i, tiles):
+        for j, ctr, res in residuals(P1, i, tiles):
+            new[i, rows(j), :] = (1.0 + ALPHA) * ctr - ALPHA * old[i, rows(j), :] + BETA * INV[i, rows(j), :] * res
+
+    def exchange_pressure(field, width, slot, meanwhile=None):
         per = 8 // (2 if width == 2 else 4)
         span = 8 // per
         tiles = NX // per
@@ -412,6 +416,8 @@
                     psend.at[slot, 2 + side, far], precv.at[slot, 2 + 1 - side, 1 - far], precv.at[slot, 2 + side, far],
                 ))
         go(step)
+        if meanwhile is not None:
+            meanwhile()
         land(step)
 
         def place(side, tile, m, i):
@@ -448,8 +454,7 @@
 
     def restrict(field, i):
         x = i - W
-        for j in range(1, TILES - 1):
-            _, res = residual(field, i, j)
+        for j, _, res in residuals(field, i, tuple(range(1, TILES - 1))):
             t = j - 1
             for k in range(2):
                 scaled = PR[k, x, 8 * t:8 * t + 8, :] * res
@@ -474,11 +479,11 @@
                 piece, put, get = src.at[give], dst.at[(2 - dx, 2 - dy) + give], dst.at[(2 + dx, 2 + dy) + take]
             else:
                 piece, put, get = src, dst.at[2 - dx, 2 - dy], dst.at[2 + dx, 2 + dy]
-            out.append(moved(
+            out.append(((2 * abs(dy) + abs(dx)), moved(
                 (dx, dy), piece, put, get, wsend.at[3 + parity, n], wrecv.at[3 + parity, 23 - n],
                 wrecv.at[3 + parity, n],
-            ))
-        return out
+            )))
+        return [entry for _, entry in sorted(out, key=lambda pair: -pair[0])]
 
     def jacobi(table):
         for m in range(8):
@@ -550,15 +555,15 @@
 
         for o in range(9):
             ox, oy = o // 3, o % 3
+            at = jnp.concatenate([ENT[o, h, 16:24, :] for h in range(2)], axis=0).astype(jnp.int32)
+            base = pick_from([lambda r=r: BASE[o, r:r + 1, :] for r in range(8)], at)
+            at = jnp.concatenate([ENT[o, h, 0:8, :] for h in range(2)], axis=0).astype(jnp.int32)
+            got = pick_from(
+                [lambda r=r: T25[ox + r // 24, oy + (r // 8) % 3, r % 8:r % 8 + 1, :] for r in range(72)], at
+            )
             for h in range(2):
-                at = ENT[o, h, 16:24, :].astype(jnp.int32)
-                base = pick_from([lambda r=r: BASE[o, r:r + 1, :] for r in range(8)], at)
-                at = ENT[o, h, 0:8, :].astype(jnp.int32)
-                got = pick_from(
-                    [lambda r=r: T25[ox + r // 24, oy + (r // 8) % 3, r % 8:r % 8 + 1, :] for r in range(72)], at
-                )
-                coupled = jnp.sum(got * ENT[o, h, 8:16, :], axis=0, keepdims=True)
-                LIST[o, h:h + 1, :] = base[0:1, :] - omega * coupled
+                coupled = jnp.sum(got[8 * h:8 * h + 8] * ENT[o, h, 8:16, :], axis=0, keepdims=True)
+                LIST[o, h:h + 1, :] = base[8 * h:8 * h + 1, :] - omega * coupled
 
         for r4 in range(4):
             VT[8 * r4:8 * r4 + 8, :] = pick_from(
@@ -566,8 +571,8 @@
             )
         VT[...] = VT[...].T
 
-        def correct(x):
-            for t in range(4):
+        def correct(x, blocks):
+            for t in blocks:
                 total = field[x + W, T + 8 * t:T + 8 * t + 8, :]
                 for k in range(2):
                     which = jnp.full((8, 128), 16 * k, jnp.int32) + x
@@ -580,7 +585,11 @@
                     total = total + PR[k, x, 8 * t:8 * t + 8, :] * jnp.concatenate(spread, axis=1)
                 field[x + W, T + 8 * t:T + 8 * t + 8, :] = total
 
-        loop(0, NX, correct)
+        for lo in (0, NX - 2):
+            correct(lo, range(4))
+            correct(lo + 1, range(4))
+        loop(2, NX - 2, lambda x: correct(x, (0, 3)))
+        return lambda: loop(2, NX - 2, lambda x: correct(x, (1, 2)))
 
     VT[...] = jnp.zeros_like(VT)
     for cycle in range(CYCLES):
@@ -593,8 +602,8 @@
             sweep(2, functools.partial(sweep_a, field))
             sweep(1, functools.partial(sweep_b, field, field))
         loop(W, W + NX, functools.partial(restrict, field))
-        coarse(field, cycle)
-        exchange_pressure(field, 2, 0)
+        rest = coarse(field, cycle)
+        exchange_pressure(field, 2, 0, rest)
         sweep(1, functools.partial(sweep_a, field))
         sweep(0, functools.partial(sweep_b, field, P2))
     back = pltpu.make_async_copy(P2.at[center], out_h, in_sem.at[0])
@@ -656,7 +665,7 @@
             pltpu.SemaphoreType.DMA((5, 24)),
         ],
         compiler_params=pltpu.CompilerParams(
-            collective_id=0, has_side_effects=True, vmem_limit_bytes=52 << 20
+            collective_id=0, has_side_effects=True, vmem_limit_bytes=63 << 20
         ),
     )(rhs, perm_h, perm_v, prolong, blk_slot, recv_slot.T, coarse_cols, coarse_off, coarse_diag)
 

time: 121 us -> 107 us (0.88); the launches traced: 121 us -> 106 us
  Pallas kernels: 117 us -> 104 us
  local copies, waits for them, and re-layouts: 4.59 us -> 2.29 us
    pallas_call x1, Pallas kernels: 117 us -> 104 us  [shards(): pl.pallas_call(kernel, out_shape=jax.ShapeDtypeStruct(rhs.shape, f32), in...]
    unnamed x11 -> x1, local copies, waits for them, and re-layouts: 4.59 us -> 2.29 us
where the time goes in v3:
time: 107 us; the launch traced here: 106 us
  Pallas kernels  104 us (97%)
  local copies, waits for them, and re-layouts  2.29 us (2%)
    pallas_call x1, Pallas kernels, shards(): pl.pallas_call(kernel, out_shape=jax.ShapeDtypeStruct(rhs.shape, f32), in...  104 us
    unnamed x1, local copies, waits for them, and re-layouts  2.29 us

profile of v3, /device:TPU:7, one launch (start us, length us, event | category | flops | bytes accessed | tf_op | source)
XLA Modules:
  0.0 105.9 jit_solution(8037946741543856842)
XLA Ops:
  0.0 103.6 %shard_map.91 = f32[16,32,512]{2,1,0:T(8,128)} custom-call(f32[16,32,512]{2,1,0:T(8,128)} %rhs_h.1, f32[16,32,512]{2,1,0:T(8,128)} %ph_h.1, f32[16,32,512]{2,1,0:T(8,128)} %pv_h.1, f32[2,16,32,512]{3,2,1,0:T(8,128)} %pr_h.1, s32[2,16,128]{2,1,0:T(8,128)} %slot_h.1, s32[1,2304]{1,0:T(1,128)} %bitcast.1, s32[8,1024]{1,0:T(8,128)} %cols_h.1, f32[8,1024]{1,0:T(8,128)} %off_h.1, ...), custom_call_target="tpu_custom_call" | custom-call | tf_op jit(solution)/shard_map/pallas_call | solution.py:618
  103.6 2.3 %copy.11 = f32[16,32,512]{2,1,0:T(8,128)} copy(f32[16,32,512]{2,1,0:T(8,128)} %shard_map.91) | data formatting | bytes 2097152

commit v4 on v3

--- a/solution.py
+++ b/solution.py
@@ -57,11 +57,12 @@
     )
 
 
-def pick_from(table_rows, at):
+def pick_from(table_rows, at, got=None, chosen=None):
     high = at >> 7
-    got = jnp.zeros(at.shape, f32)
+    got = jnp.zeros(at.shape, f32) if got is None else got
     for r, row in enumerate(table_rows):
-        got = jnp.where(high == r, pick(row(), at), got)
+        if chosen is None or r in chosen:
+            got = jnp.where(high == r, pick(row(), at), got)
     return got
 
 
@@ -69,7 +70,7 @@
     rhs_h, ph_h, pv_h, pr_h, slot_h, recv_h, cols_h, off_h, diag_h, out_h,
     RHS, PH, PV, TE, TN, TU, INV, P0, P1, P2, PR, PKS, RKS, PKP, RKP, RKC,
     WH, WL, HOT, LHOT, AB, SLOT, LT, VT, RIDX, INVN, DIAN, MSG, ENT,
-    OUT, ARR, RATN, TAB, T25, LIST, Y, BASE,
+    OUT, ARR, RATN, TAB, T25, LIST, Y, BASE, LASTB, LASTG,
     slot_r, recv_r, cols_r, off_r, diag_r,
     in_sem, fsend, frecv, psend, precv, csend, crecv, wsend, wrecv,
 ):
@@ -276,7 +277,6 @@
         tables.append(moved(to, INVN.at[4], INVN.at[8 - o], INVN.at[o], wsend.at[0, o], wrecv.at[0, 8 - o], wrecv.at[0, o]))
         tables.append(moved(to, DIAN.at[4], DIAN.at[8 - o], DIAN.at[o], wsend.at[1, o], wrecv.at[1, 8 - o], wrecv.at[1, o]))
     tables += around(lambda o: MSG.at[o], ENT, wsend.at[2], wrecv.at[2])
-    go(tables)
 
     LT[...] = jnp.zeros_like(LT)
     LT[0:32, :] = SLOT[...] & 127
@@ -312,13 +312,16 @@
             down = TN[i, 8 * j - 1:8 * j + 7, :] if j > 0 else pltpu.roll(tn, 1, 0)
             tu = TU[i, rows(j), :]
             total = storage_coef + TE[i, rows(j), :] + TE[i - 1, rows(j), :] + tn + down + tu + pltpu.roll(tu, 1, 1)
-            INV[i, rows(j), :] = inverse(total)
+            inv = inverse(total)
+            INV[i, rows(j), :] = inv
+            P1[i, rows(j), :] = (1.0 / THETA) * inv * RHS[i, rows(j), :]
 
     every = tuple(range(TILES))
     loop(W, W + NX - 1, lambda i: edge_x(i, (1, 2, 3, 4)))
     loop(W + 1, W + NX - 1, lambda i: edge_yz(i, (1, 2, 3), (2, 3)))
 
     land(first)
+    go(tables)
 
     def unpack_first(i):
         got = RKS[0, i - 1]
@@ -365,10 +368,6 @@
         tiles = tuple(range(TILES)) if extent > 0 else tuple(range(1, TILES - 1))
         loop(W - extent, W + NX + extent, lambda i: update(i, tiles))
 
-    def start_from_zero(i, tiles):
-        for j in tiles:
-            P1[i, rows(j), :] = (1.0 / THETA) * INV[i, rows(j), :] * RHS[i, rows(j), :]
-
     def sweep_a(field, i, tiles):
         for j, ctr, res in residuals(field, i, tiles):
             P1[i, rows(j), :] = ctr + (1.0 / THETA) * INV[i, rows(j), :] * res
@@ -479,16 +478,26 @@
                 piece, put, get = src.at[give], dst.at[(2 - dx, 2 - dy) + give], dst.at[(2 + dx, 2 + dy) + take]
             else:
                 piece, put, get = src, dst.at[2 - dx, 2 - dy], dst.at[2 + dx, 2 + dy]
-            out.append(((2 * abs(dy) + abs(dx)), moved(
+            outer = max(abs(dx), abs(dy)) == 2
+            out.append(((10 * outer + 2 * abs(dy) + abs(dx)), moved(
                 (dx, dy), piece, put, get, wsend.at[3 + parity, n], wrecv.at[3 + parity, 23 - n],
                 wrecv.at[3 + parity, n],
             )))
         return [entry for _, entry in sorted(out, key=lambda pair: -pair[0])]
 
-    def jacobi(table):
+    def jacobi(table, near, far):
+        every_row = [lambda r=r: table[r // 8, r % 8:r % 8 + 1, :] for r in range(72)]
+        corner = [r for r in range(72) if r // 8 in (0, 2, 6, 8)]
+        side = [r for r in range(72) if r // 8 not in (0, 2, 6, 8)]
+        near()
+        partly = []
         for m in range(8):
             at = cols_r[:, 128 * m:128 * m + 128]
-            got = pick_from([lambda r=r: table[r // 8, r % 8:r % 8 + 1, :] for r in range(72)], at)
+            partly.append(pick_from(every_row, at, None, side))
+        far()
+        for m in range(8):
+            at = cols_r[:, 128 * m:128 * m + 128]
+            got = pick_from(every_row, at, partly[m], corner)
             coupled = jnp.sum(got * off_r[:, 128 * m:128 * m + 128], axis=0, keepdims=True)
             mine = table[4, m:m + 1, :]
             Y[m:m + 1, :] = mine + omega * (RATN[4, m:m + 1, :] - mine - coupled)
@@ -538,32 +547,42 @@
             ratio = total * DIAN[p]
             RATN[p] = ratio
             TAB[0, p] = omega * ratio
-        jacobi(TAB.at[0])
+        jacobi(TAB.at[0], lambda: None, lambda: None)
         for s in range(1, CJ - 1):
             table = TAB.at[s % 2]
             step = around(lambda o: Y, table, csend.at[s % 2], crecv.at[s % 2])
             go(step)
             table[4] = Y[...]
-            land(step)
-            jacobi(table)
+            jacobi(table, lambda: land(step[4:]), lambda: land(step[:4]))
         step = wide(Y, T25, 1, False)
         go(step)
         T25[2, 2] = Y[...]
-        land(step)
+        land(step[16:])
         for o in range(9):
             BASE[o] = (1.0 - omega) * T25[1 + o // 3, 1 + o % 3] + omega * RATN[o]
 
+        def last_rows(o, got, inside):
+            ox, oy = o // 3, o % 3
+            at = jnp.concatenate([ENT[o, h, 0:8, :] for h in range(2)], axis=0).astype(jnp.int32)
+            chosen = [
+                r for r in range(72)
+                if (1 <= ox + r // 24 <= 3 and 1 <= oy + (r // 8) % 3 <= 3) == inside
+            ]
+            return pick_from(
+                [lambda r=r: T25[ox + r // 24, oy + (r // 8) % 3, r % 8:r % 8 + 1, :] for r in range(72)],
+                at, got, chosen,
+            )
+
         for o in range(9):
-            ox, oy = o // 3, o % 3
             at = jnp.concatenate([ENT[o, h, 16:24, :] for h in range(2)], axis=0).astype(jnp.int32)
-            base = pick_from([lambda r=r: BASE[o, r:r + 1, :] for r in range(8)], at)
-            at = jnp.concatenate([ENT[o, h, 0:8, :] for h in range(2)], axis=0).astype(jnp.int32)
-            got = pick_from(
-                [lambda r=r: T25[ox + r // 24, oy + (r // 8) % 3, r % 8:r % 8 + 1, :] for r in range(72)], at
-            )
+            LASTB[o] = pick_from([lambda r=r: BASE[o, r:r + 1, :] for r in range(8)], at)
+            LASTG[o] = last_rows(o, None, True)
+        land(step[:16])
+        for o in range(9):
+            got = LASTG[o] if o == 4 else last_rows(o, LASTG[o], False)
             for h in range(2):
                 coupled = jnp.sum(got[8 * h:8 * h + 8] * ENT[o, h, 8:16, :], axis=0, keepdims=True)
-                LIST[o, h:h + 1, :] = base[8 * h:8 * h + 1, :] - omega * coupled
+                LIST[o, h:h + 1, :] = LASTB[o, 8 * h:8 * h + 1, :] - omega * coupled
 
         for r4 in range(4):
             VT[8 * r4:8 * r4 + 8, :] = pick_from(
@@ -595,7 +614,6 @@
     for cycle in range(CYCLES):
         field = (P0, P2)[cycle]
         if cycle == 0:
-            sweep(2, start_from_zero)
             sweep(1, sweep_b_first)
         else:
             exchange_pressure(field, 3, 1)
@@ -649,6 +667,8 @@
             pltpu.VMEM((9, 2, 128), f32),
             pltpu.VMEM((8, 128), f32),
             pltpu.VMEM((9, 8, 128), f32),
+            pltpu.VMEM((9, 16, 128), f32),
+            pltpu.VMEM((9, 16, 128), f32),
             pltpu.VMEM((2, NX, 128), i32),
             pltpu.VMEM((1, 2304), i32),
             pltpu.VMEM((8, 1024), i32),

time: 107 us -> 104 us (0.972)
  Pallas kernels: 104 us -> 101 us
    pallas_call x1, Pallas kernels: 104 us -> 101 us  [shards(): pl.pallas_call(kernel, out_shape=jax.ShapeDtypeStruct(rhs.shape, f32), in...]
where the time goes in v4:
time: 104 us; the launch traced here: 103 us
  Pallas kernels  101 us (97%)
  local copies, waits for them, and re-layouts  2.29 us (2%)
    pallas_call x1, Pallas kernels, shards(): pl.pallas_call(kernel, out_shape=jax.ShapeDtypeStruct(rhs.shape, f32), in...  101 us
    unnamed x1, local copies, waits for them, and re-layouts  2.29 us

profile of v4, /device:TPU:7, one launch (start us, length us, event | category | flops | bytes accessed | tf_op | source)
XLA Modules:
  0.0 103.5 jit_solution(8161397393570919356)
XLA Ops:
  0.0 101.2 %shard_map.91 = f32[16,32,512]{2,1,0:T(8,128)} custom-call(f32[16,32,512]{2,1,0:T(8,128)} %rhs_h.1, f32[16,32,512]{2,1,0:T(8,128)} %ph_h.1, f32[16,32,512]{2,1,0:T(8,128)} %pv_h.1, f32[2,16,32,512]{3,2,1,0:T(8,128)} %pr_h.1, s32[2,16,128]{2,1,0:T(8,128)} %slot_h.1, s32[1,2304]{1,0:T(1,128)} %bitcast.1, s32[8,1024]{1,0:T(8,128)} %cols_h.1, f32[8,1024]{1,0:T(8,128)} %off_h.1, ...), custom_call_target="tpu_custom_call" | custom-call | tf_op jit(solution)/shard_map/pallas_call | solution.py:636
  101.2 2.3 %copy.11 = f32[16,32,512]{2,1,0:T(8,128)} copy(f32[16,32,512]{2,1,0:T(8,128)} %shard_map.91) | data formatting | bytes 2097152

commit v5 on v4

--- a/solution.py
+++ b/solution.py
@@ -68,7 +68,7 @@
 
 def kernel(
     rhs_h, ph_h, pv_h, pr_h, slot_h, recv_h, cols_h, off_h, diag_h, out_h,
-    RHS, PH, PV, TE, TN, TU, INV, P0, P1, P2, PR, PKS, RKS, PKP, RKP, RKC,
+    RHS, PH, PV, TE, TN, TU, INV, P0, P1, P2, PR, PKS, PKC, RKS, PKP, RKP, RKC,
     WH, WL, HOT, LHOT, AB, SLOT, LT, VT, RIDX, INVN, DIAN, MSG, ENT,
     OUT, ARR, RATN, TAB, T25, LIST, Y, BASE, LASTB, LASTG,
     slot_r, recv_r, cols_r, off_r, diag_r,
@@ -103,17 +103,17 @@
         def _():
             pl.semaphore_signal(bar, inc=1, device_id=(x, y), device_id_type=MESH)
 
-    def loop(lo, hi, fn):
-        pairs = (hi - lo) // 2
+    def loop(lo, hi, fn, per=2):
+        steps = (hi - lo) // per
 
         def body(n, carry):
-            fn(lo + 2 * n)
-            fn(lo + 2 * n + 1)
+            for q in range(per):
+                fn(lo + per * n + q)
             return carry
 
-        lax.fori_loop(0, pairs, body, 0)
-        if (hi - lo) % 2:
-            fn(hi - 1)
+        lax.fori_loop(0, steps, body, 0)
+        for i in range(lo + per * steps, hi):
+            fn(i)
 
     def clear(view):
         def one(i):
@@ -160,6 +160,9 @@
         PKS[1, x] = jnp.where(sub512 >= 5, a, jnp.where(sub512 >= 3, pltpu.roll(b, 5, 0), pltpu.roll(c, 3, 0)))
 
     loop(0, NX, pack_first)
+    for far, near_x, next_x in ((0, 0, 1), (1, NX - 1, NX - 2)):
+        PKC[0, far] = jnp.where(sub512 == 7, pltpu.roll(PKS[0, next_x], 7, 0), PKS[0, near_x])
+        PKC[1, far] = jnp.where(sub512 == 0, pltpu.roll(PKS[1, next_x], 1, 0), PKS[1, near_x])
 
     peers = sum(neighbour(o // 3 - 1, o % 3 - 1)[2].astype(jnp.int32) for o in AROUND)
     pl.semaphore_wait(bar, peers)
@@ -206,11 +209,11 @@
     for dy in (-1, 1):
         side = (dy + 1) // 2
         for dx in (0, -1, 1):
-            src = {0: pl.ds(0, NX), -1: pl.ds(0, 2), 1: pl.ds(NX - 2, 2)}[dx]
-            put = {0: pl.ds(2, NX), -1: pl.ds(NX + 2, 2), 1: pl.ds(0, 2)}[dx]
-            get = {0: pl.ds(2, NX), -1: pl.ds(0, 2), 1: pl.ds(NX + 2, 2)}[dx]
+            src = PKS.at[side] if dx == 0 else PKC.at[side, (dx + 1) // 2]
+            put = {0: pl.ds(2, NX), -1: NX + 2, 1: 1}[dx]
+            get = {0: pl.ds(2, NX), -1: 1, 1: NX + 2}[dx]
             first.append(moved(
-                (dx, dy), PKS.at[side, src], RKS.at[1 - side, put], RKS.at[side, get],
+                (dx, dy), src, RKS.at[1 - side, put], RKS.at[side, get],
                 fsend.at[3, dx + 1 + 3 * side], frecv.at[3, 1 - dx + 3 * (1 - side)],
                 frecv.at[3, dx + 1 + 3 * side],
             ))
@@ -322,6 +325,9 @@
 
     land(first)
     go(tables)
+    for near_x, next_x in ((1, 0), (NX + 2, NX + 3)):
+        RKS[0, next_x] = pltpu.roll(RKS[0, near_x], 7, 0)
+        RKS[1, next_x] = pltpu.roll(RKS[1, near_x], 1, 0)
 
     def unpack_first(i):
         got = RKS[0, i - 1]
@@ -607,8 +613,8 @@
         for lo in (0, NX - 2):
             correct(lo, range(4))
             correct(lo + 1, range(4))
-        loop(2, NX - 2, lambda x: correct(x, (0, 3)))
-        return lambda: loop(2, NX - 2, lambda x: correct(x, (1, 2)))
+        loop(2, NX - 2, lambda x: correct(x, (0, 3)), 4)
+        return lambda: loop(2, NX - 2, lambda x: correct(x, (1, 2)), 4)
 
     VT[...] = jnp.zeros_like(VT)
     for cycle in range(CYCLES):
@@ -642,6 +648,7 @@
         + [
             pltpu.VMEM((2, NX, NY, NZ), f32),
             pltpu.VMEM((2, NX, 8, NZ), f32),
+            pltpu.VMEM((2, 2, 8, NZ), f32),
             pltpu.VMEM((2, NX + 4, 8, NZ), f32),
             pltpu.VMEM((2, 8, 8, NZ), f32),
             pltpu.VMEM((2, 2, 8, 8, NZ), f32),

time: 104 us -> 103 us (level)
  no operation moved by 1% of the time
where the time goes in v5:
time: 103 us
  Pallas kernels  101 us (98%)
  local copies, waits for them, and re-layouts  2.29 us (2%)
    pallas_call x1, Pallas kernels, shards(): pl.pallas_call(kernel, out_shape=jax.ShapeDtypeStruct(rhs.shape, f32), in...  101 us
    unnamed x1, local copies, waits for them, and re-layouts  2.29 us

profile of v5, /device:TPU:7, one launch (start us, length us, event | category | flops | bytes accessed | tf_op | source)
XLA Modules:
  0.0 102.9 jit_solution(16301490605457285876)
XLA Ops:
  0.0 100.6 %shard_map.91 = f32[16,32,512]{2,1,0:T(8,128)} custom-call(f32[16,32,512]{2,1,0:T(8,128)} %rhs_h.1, f32[16,32,512]{2,1,0:T(8,128)} %ph_h.1, f32[16,32,512]{2,1,0:T(8,128)} %pv_h.1, f32[2,16,32,512]{3,2,1,0:T(8,128)} %pr_h.1, s32[2,16,128]{2,1,0:T(8,128)} %slot_h.1, s32[1,2304]{1,0:T(1,128)} %bitcast.1, s32[8,1024]{1,0:T(8,128)} %cols_h.1, f32[8,1024]{1,0:T(8,128)} %off_h.1, ...), custom_call_target="tpu_custom_call" | custom-call | tf_op jit(solution)/shard_map/pallas_call | solution.py:642
  100.6 2.3 %copy.11 = f32[16,32,512]{2,1,0:T(8,128)} copy(f32[16,32,512]{2,1,0:T(8,128)} %shard_map.91) | data formatting | bytes 2097152

commit v6 on v5

--- a/solution.py
+++ b/solution.py
@@ -405,7 +405,7 @@
             PKP[1, g] = b
 
         loop(0, tiles, pack)
-        step = x_strips(field, field, W, width, psend.at[slot, 0], precv.at[slot, 0])
+        step = []
         for dy in (-1, 1):
             side = (dy + 1) // 2
             step.append(moved(
@@ -420,6 +420,7 @@
                     RKC.at[slot, side, far],
                     psend.at[slot, 2 + side, far], precv.at[slot, 2 + 1 - side, 1 - far], precv.at[slot, 2 + side, far],
                 ))
+        step += x_strips(field, field, W, width, psend.at[slot, 0], precv.at[slot, 0])
         go(step)
         if meanwhile is not None:
             meanwhile()

time: 103 us -> 102 us (level)
  Pallas kernels: 101 us -> 99.9 us
where the time goes in v6:
time: 102 us
  Pallas kernels  99.9 us (98%)
  local copies, waits for them, and re-layouts  2.29 us (2%)
    pallas_call x1, Pallas kernels, shards(): pl.pallas_call(kernel, out_shape=jax.ShapeDtypeStruct(rhs.shape, f32), in...  99.9 us
    unnamed x1, local copies, waits for them, and re-layouts  2.29 us

profile of v6, /device:TPU:7, one launch (start us, length us, event | category | flops | bytes accessed | tf_op | source)
XLA Modules:
  0.0 102.2 jit_solution(2242525766343545607)
XLA Ops:
  0.0 99.9 %shard_map.91 = f32[16,32,512]{2,1,0:T(8,128)} custom-call(f32[16,32,512]{2,1,0:T(8,128)} %rhs_h.1, f32[16,32,512]{2,1,0:T(8,128)} %ph_h.1, f32[16,32,512]{2,1,0:T(8,128)} %pv_h.1, f32[2,16,32,512]{3,2,1,0:T(8,128)} %pr_h.1, s32[2,16,128]{2,1,0:T(8,128)} %slot_h.1, s32[1,2304]{1,0:T(1,128)} %bitcast.1, s32[8,1024]{1,0:T(8,128)} %cols_h.1, f32[8,1024]{1,0:T(8,128)} %off_h.1, ...), custom_call_target="tpu_custom_call" | custom-call | tf_op jit(solution)/shard_map/pallas_call | solution.py:643
  100.0 2.3 %copy.11 = f32[16,32,512]{2,1,0:T(8,128)} copy(f32[16,32,512]{2,1,0:T(8,128)} %shard_map.91) | data formatting | bytes 2097152
